TPU v7x, 256 devices: a whole 4x4x8 slice. The times are simulated.
256 devices in a mesh: expert: 64 (over x, z, core), fsdp: 4 (over y).
Axes of the slice: x: 4, y: 4, z: 8, core: 2. Of those that a mesh axis runs over, the one named last changes fastest.
Arguments:
- teacher_in: bfloat16 [8192, 4096], P('expert'), may hold values from -6 to 6
- routes: int32 [8192, 8], P('expert'), may hold values from 0 to 63, all different within a row; in each aligned block of 128 rows (0 to 127, 128 to 255, ...) at most 18 rows name the same one
- route_weights: float32 [8192, 8], P('expert'), may hold values from 0.1 to 0.5
- expert_gate_up: bfloat16 [64, 4096, 2, 1024], P('expert', None, None, 'fsdp'), may hold values from -0.09375 to 0.09375
- expert_down: bfloat16 [64, 1024, 4096], P('expert', 'fsdp'), may hold values from -0.1875 to 0.1875
- student_in: bfloat16 [8192, 2048], P('expert'), may hold values from -16 to 16
- norm_gain: float32 [2048], replicated, may hold values from 0.5 to 2
- projector: bfloat16 [2048, 4096], P(None, 'fsdp'), may hold values from -0.125 to 0.125
- second_moment: float32 [2048, 4096], P('expert', 'fsdp'), may hold values from 2048 to 32768
Outputs:
- d_student: bfloat16 [8192, 2048], P('expert')
- proj_step: float32 [2048, 4096], P('expert', 'fsdp')
Inputs may be any that keep to these rules, and one draw needn't show every extreme that they name: `routes`: each row names 8 different experts; in each block of 128 consecutive rows (the rows of one index of expert) no expert is named by more than 18 rows.
All inputs are finite; a program needn't handle non-finite values.
Results may differ from a plain program's by a relative error of at most 0.02.
Values may be sent and summed in bfloat16 or wider, within the bound.
A program may use at most 128 MiB of HBM per device.

v0:
```python
import jax
import jax.numpy as jnp
from jax import lax
from jax.sharding import PartitionSpec as P

beta_two = 0.95


def slot_targets(routes, experts, capacity):
    flatten = routes.reshape(-1)
    onehot = (flatten[:, None] == jnp.arange(experts, dtype=jnp.int32)[None, :]).astype(jnp.int32)
    before = jnp.cumsum(onehot, axis=0) - onehot
    position = jnp.sum(before * onehot, axis=1)
    return flatten * capacity + position


def expert_rows(received, gate_up, down_rows):
    sources, slot_count, columns = received.shape
    token_rows = received.reshape(sources * slot_count, columns)
    half_width = down_rows.shape[0]
    gate_up_out = jnp.dot(token_rows, gate_up, preferred_element_type=jnp.float32)
    hidden = (jax.nn.silu(gate_up_out[:, :half_width]) * gate_up_out[:, half_width:]).astype(
        jnp.bfloat16
    )
    expert_out = jnp.dot(hidden, down_rows, preferred_element_type=jnp.float32)
    return expert_out.reshape(sources, slot_count, down_rows.shape[1])


def finish_slots(expert_out):
    return expert_out.astype(jnp.bfloat16)


def combine_rows(returned, targets, route_weights):
    flatten = returned.reshape(-1, returned.shape[2])
    picked = flatten[targets].reshape(
        route_weights.shape[0], route_weights.shape[1], returned.shape[2]
    )
    return jnp.sum(picked.astype(jnp.float32) * route_weights[:, :, None], axis=1)


def per_device(
    teacher_in,
    routes,
    route_weights,
    expert_gate_up,
    expert_down,
    student_in,
    norm_gain,
    projector,
    second_moment,
):
    tokens_here = teacher_in.shape[0]
    model_width = teacher_in.shape[1]
    top_count = routes.shape[1]
    experts = lax.axis_size("expert")
    capacity = min(tokens_here, tokens_here * top_count * 9 // (8 * experts))
    targets = slot_targets(routes, experts, capacity)
    token_ids = jnp.arange(tokens_here * top_count, dtype=jnp.int32) // top_count
    slot_token = jnp.full((experts * capacity,), tokens_here, jnp.int32).at[targets].set(token_ids)
    gate_up = expert_gate_up.reshape(expert_gate_up.shape[1], -1)
    down_rows = expert_down[0]
    padded = jnp.concatenate([teacher_in, jnp.zeros((1, model_width), teacher_in.dtype)], axis=0)
    buffer = padded[slot_token].reshape(experts, capacity, model_width)
    results = finish_slots(
        expert_rows(
            lax.all_to_all(buffer, "expert", split_axis=0, concat_axis=0, tiled=True),
            gate_up,
            down_rows,
        )
    )
    returned = lax.all_to_all(results, "expert", split_axis=0, concat_axis=0, tiled=True)
    teacher = lax.psum_scatter(
        combine_rows(returned, targets, route_weights).astype(jnp.bfloat16),
        "fsdp",
        scatter_dimension=1,
        tiled=True,
    ).astype(jnp.float32)
    student_wide = student_in.astype(jnp.float32)
    inv_rms = lax.rsqrt(jnp.mean(student_wide * student_wide, axis=1, keepdims=True) + 1e-06)
    normed = student_wide * inv_rms
    student_feat = (normed * norm_gain[None, :]).astype(jnp.bfloat16)
    residue = (
        jnp.dot(student_feat, projector, preferred_element_type=jnp.float32) - teacher
    ).astype(jnp.bfloat16)
    feat_part = jnp.einsum("tc,dc->td", residue, projector, preferred_element_type=jnp.float32)
    feat_grad = lax.psum(feat_part.astype(jnp.bfloat16), "fsdp").astype(jnp.float32)
    scaled = feat_grad * norm_gain[None, :]
    d_student = (
        inv_rms * (scaled - normed * jnp.mean(scaled * normed, axis=1, keepdims=True))
    ).astype(jnp.bfloat16)
    grad_block = lax.psum_scatter(
        jnp.einsum("tr,tc->rc", student_feat, residue, preferred_element_type=jnp.float32),
        "expert",
        scatter_dimension=0,
        tiled=True,
    )
    proj_step = grad_block / jnp.sqrt(
        beta_two * second_moment + (1.0 - beta_two) * grad_block * grad_block
    )
    return (d_student, proj_step)


def solution(mesh):
    placed = (
        P("expert", None),
        P("expert", None),
        P("expert", None),
        P("expert", None, None, "fsdp"),
        P("expert", "fsdp", None),
        P("expert", None),
        P(),
        P(None, "fsdp"),
        P("expert", "fsdp"),
    )
    return jax.shard_map(
        per_device,
        mesh=mesh,
        in_specs=placed,
        out_specs=(P("expert", None), P("expert", "fsdp")),
        check_vma=False,
    )
```

profile of v0, /device:TPU:8, one launch (start us, length us, event | category | flops | bytes accessed | tf_op | source)
XLA Modules:
  0.0 961.3 jit_solution(18266899832249820295)
XLA Ops:
  7.2 0.9 copy.22
  8.3 0.7 broadcast_multiply_fusion
  9.0 18.0 %reduce-window.6 = s32[64,8,128]{2,1,0:T(8,128)S(1)} reduce-window(s32[64,8,128]{2,1,0:T(8,128)S(1)} %fusion.17, s32[]{:T(128)} %constant.40.clone.1), window={size=1x1x128 pad=0_0x0_0x127_0}, to_apply=%region_1.2 | reduce-window | flops 8323072 | bytes 524292 | tf_op jit(solution)/shard_map/reduce-window
  27.9 4.3 scatter_custom_fusion
  32.2 1.3 concatenate.3
  33.6 8.0 gather_fusion
  41.6 13.9 %reshape.82 = bf16[64,18,4096]{2,1,0:T(8,128)(2,1)} reshape(bf16[1152,4096]{1,0:T(8,128)(2,1)} %gather_fusion) | data formatting | bytes 18874368 | tf_op jit(solution)/shard_map/reshape | solution.py:63
  55.5 12.3 %all-to-all-start = ((bf16[64,18,4096]{2,1,0:T(8,128)(2,1)}), bf16[64,18,4096]{2,1,0:T(8,128)(2,1)}, u32[]{:S(2)}, u32[]{:S(2)}) async-start(bf16[64,18,4096]{2,1,0:T(8,128)(2,1)} %reshape.82), calls=%async_computation | async-start | bytes 25165824 | tf_op jit(solution)/shard_map/all_to_all | solution.py:66
  67.8 4.9 copy.30
  72.7 269.7 %all-to-all-done = bf16[64,18,4096]{2,1,0:T(8,128)(2,1)} async-done(((bf16[64,18,4096]{2,1,0:T(8,128)(2,1)}), bf16[64,18,4096]{2,1,0:T(8,128)(2,1)}, u32[]{:S(2)}, u32[]{:S(2)}) %all-to-all-start) | async-done | bytes 9437216 | tf_op jit(solution)/shard_map/all_to_all | solution.py:66
  342.5 14.1 %reshape.83 = bf16[1152,4096]{1,0:T(8,128)(2,1)} reshape(bf16[64,18,4096]{2,1,0:T(8,128)(2,1)} %all-to-all-done) | data formatting | bytes 18874368 | tf_op jit(solution)/shard_map/reshape | solution.py:19
  356.6 8.8 fusion.29
  365.4 0.3 fusion.6
  365.9 2.8 convolution_convert_fusion
  368.8 20.4 %copy.27 = bf16[64,18,4096]{2,1,0:T(8,128)(2,1)} copy(bf16[64,18,4096]{2,0,1:T(8,128)(2,1)S(1)} %convolution_convert_fusion) | data formatting | bytes 18874368 | tf_op jit(solution)/shard_map/convert_element_type | solution.py:30
  389.2 7.1 all-to-all-start.1
  396.3 0.3 reduce-scatter.3.cloned.1.call-start
  396.7 274.4 %all-to-all-done.1 = bf16[64,18,4096]{2,1,0:T(8,128)(2,1)} async-done(((bf16[64,18,4096]{2,1,0:T(8,128)(2,1)}), bf16[64,18,4096]{2,1,0:T(8,128)(2,1)}, u32[]{:S(2)}, u32[]{:S(2)}) %all-to-all-start.1) | async-done | bytes 9437216 | tf_op jit(solution)/shard_map/all_to_all | solution.py:71
  671.1 14.1 %reshape.85 = bf16[1152,4096]{1,0:T(8,128)(2,1)} reshape(bf16[64,18,4096]{2,1,0:T(8,128)(2,1)} %all-to-all-done.1) | data formatting | bytes 18874368 | tf_op jit(solution)/shard_map/reshape | solution.py:34
  685.2 20.0 %gather_fusion.1 = bf16[1024,4096]{1,0:T(8,128)(2,1)} fusion(bf16[1152,4096]{1,0:T(8,128)(2,1)} %reshape.85, s32[1024]{0:T(1024)S(1)} %broadcast_clamp_fusion), kind=kCustom, calls=%fused_computation.1 | custom fusion | bytes 16781312 | tf_op jit(solution)/shard_map/gather | solution.py:35
  705.2 13.0 %fusion = bf16[128,4096]{1,0:T(8,128)(2,1)} fusion(bf16[1024,4096]{1,0:T(8,128)(2,1)} %gather_fusion.1, f32[128,8]{1,0:T(8,128)S(1)} %copy.28), kind=kLoop, calls=%fused_computation.4 | loop fusion | flops 12058624 | bytes 9441280 | tf_op jit(solution)/shard_map/reduce_sum | solution.py:38
  718.2 0.3 all-reduce.3.cloned.1.call-start
  718.7 21.5 %reduce-scatter.3.cloned.1.call-done = bf16[128,1024]{1,0:T(8,128)(2,1)} async-done(((bf16[128,4096]{1,0:T(8,128)(2,1)}), bf16[128,1024]{1,0:T(8,128)(2,1)}) %reduce-scatter.3.cloned.1.call-update) | async-done | bytes 262160 | tf_op jit(solution)/shard_map/reduce_scatter | solution.py:72
  740.2 3.1 fusion.5
  743.3 0.4 copy-done.2
  743.7 2.3 convolution_convert_fusion.1
  746.1 4.6 fusion.18
  750.7 44.4 %all-reduce.3.cloned.1.call-done = bf16[128,2048]{1,0:T(8,128)(2,1)} async-done(((bf16[128,2048]{1,0:T(8,128)(2,1)}), bf16[128,2048]{1,0:T(8,128)(2,1)}) %all-reduce.3.cloned.1.call-update) | async-done | bytes 524304 | tf_op jit(solution)/shard_map/psum | solution.py:86
  795.1 1.4 fusion.8
  796.5 2.2 fusion.11
  798.7 154.5 %reduce-scatter.5.cloned.1.call-done = f32[32,1024]{1,0:T(8,128)} async-done(((f32[2048,1024]{1,0:T(8,128)}), f32[32,1024]{1,0:T(8,128)}) %reduce-scatter.5.cloned.1.call-update) | async-done | bytes 131088 | tf_op jit(solution)/shard_map/reduce_scatter | solution.py:91
  953.1 1.6 fusion.23
  (39 shorter events, 1.6 us)
Async XLA Ops:
  7.2 358.8 %copy-start = (bf16[1,256,4096]{2,1,0:T(8,128)(2,1)S(1)}, bf16[1,256,4096]{2,1,0:T(8,128)(2,1)}, u32[]{:S(2)}) copy-start(bf16[1,256,4096]{2,1,0:T(8,128)(2,1)} %param.13) | copy-start | bytes 6291460
  55.5 287.0 %all-to-all-start = ((bf16[64,18,4096]{2,1,0:T(8,128)(2,1)}), bf16[64,18,4096]{2,1,0:T(8,128)(2,1)}, u32[]{:S(2)}, u32[]{:S(2)}) async-start(bf16[64,18,4096]{2,1,0:T(8,128)(2,1)} %reshape.82), calls=%async_computation | async-start | bytes 25165824 | tf_op jit(solution)/shard_map/all_to_all | solution.py:66
  389.2 7.4 copy-start.6
  389.2 281.9 %all-to-all-start.1 = ((bf16[64,18,4096]{2,1,0:T(8,128)(2,1)}), bf16[64,18,4096]{2,1,0:T(8,128)(2,1)}, u32[]{:S(2)}, u32[]{:S(2)}) async-start(bf16[64,18,4096]{2,1,0:T(8,128)(2,1)} %copy.27), calls=%async_computation.1 | async-start | bytes 25165824 | tf_op jit(solution)/shard_map/all_to_all | solution.py:71
  396.3 343.9 %reduce-scatter.3.cloned.1.call-start = ((), (), s32[]{:S(2)}) async-start(), calls=%async_computation.4 | async-start | bytes 1310720 | tf_op jit(solution)/shard_map/reduce_scatter | solution.py:72
  705.2 13.4 %copy-start.3 = (bf16[128,2048]{1,0:T(8,128)(2,1)S(1)}, bf16[128,2048]{1,0:T(8,128)(2,1)}, u32[]{:S(2)}) copy-start(bf16[128,2048]{1,0:T(8,128)(2,1)} %param.14) | copy-start | bytes 1572868
  705.2 35.0 %copy-start.4 = (f32[2048]{0:T(1024)S(1)}, f32[2048]{0:T(1024)}, u32[]{:S(2)}) copy-start(f32[2048]{0:T(1024)} %param.15) | copy-start | bytes 24580
  718.2 76.9 %all-reduce.3.cloned.1.call-start = ((), (), s32[]{:S(2)}) async-start(), calls=%async_computation.5 | async-start | bytes 1048576 | tf_op jit(solution)/shard_map/psum | solution.py:86
  740.2 3.5 copy-start.2
  746.0 207.1 %reduce-scatter.5.cloned.1.call-start = ((), (), s32[]{:S(2)}) async-start(), calls=%async_computation.6 | async-start | bytes 8519680 | tf_op jit(solution)/shard_map/reduce_scatter | solution.py:91
  750.7 204.1 %copy-start.1 = (bf16[1,256,4096]{2,1,0:T(8,128)(2,1)S(1)}, bf16[1,256,4096]{2,1,0:T(8,128)(2,1)}, u32[]{:S(2)}) copy-start(bf16[1,256,4096]{2,1,0:T(8,128)(2,1)} %param.13) | copy-start | bytes 6291460
  750.7 202.5 %copy-start.5 = (f32[32,1024]{1,0:T(8,128)S(1)}, f32[32,1024]{1,0:T(8,128)}, u32[]{:S(2)}) copy-start(f32[32,1024]{1,0:T(8,128)} %param.17) | copy-start | bytes 393220
Sparse Core Ops, SparseCore 0:
  718.3 21.8 reduce-scatter.2
  746.2 48.8 all-reduce.2
  799.9 153.1 reduce-scatter.4
where the time goes:
time: 963 us; the launch traced here: 961 us
  waiting for transfers between devices  764 us (79%)
  local copies, waits for them, and re-layouts  103 us (11%)
  other arithmetic  37.7 us (4%)
  matrix products  21.7 us (2%)
  starting transfers between devices  20.1 us (2%)
  between operations  13.9 us (1%)
    all_to_all x1, waiting for transfers between devices, per_device(): lax.all_to_all(results, 'expert', split_axis=0, concat_axis=0, tiled=True)  274 us
    all_to_all x1, waiting for transfers between devices, per_device(): lax.all_to_all(buffer, 'expert', split_axis=0, concat_axis=0, tiled=True)  270 us
    reduce_scatter x1, waiting for transfers between devices, per_device(): lax.psum_scatter(jnp.einsum('tr,tc->rc', student_feat, residue, preferred...  154 us
    psum x1, waiting for transfers between devices, per_device(): lax.psum(feat_part.astype(jnp.bfloat16), 'fsdp').astype(jnp.float32)  44.4 us
    reduce_scatter x1, waiting for transfers between devices, per_device(): lax.psum_scatter(combine_rows(returned, targets, route_weights).astype(jn...  21.5 us
    convert_element_type x1, local copies, waits for them, and re-layouts, finish_slots(): return expert_out.astype(jnp.bfloat16)  20.4 us
    gather x1, local copies, waits for them, and re-layouts, combine_rows(): flatten[targets]  20 us
  transfers between devices with their start and end apart: 5, of which 5 were waited for; matrix products, arithmetic and copies ran while one was open for 1% of the time, Pallas kernels for 0%

commit v1 on v0

v1 whole, which is shorter than its diff:
```python
import jax
import jax.numpy as jnp
from jax import lax
from jax.sharding import PartitionSpec as P

beta_two = 0.95


def slot_maps(routes, route_weights, experts):
    tokens = routes.shape[0]
    named = routes[:, :, None] == jnp.arange(experts, dtype=jnp.int32)[None, None, :]
    member = jnp.any(named, axis=1)
    weight = jnp.sum(jnp.where(named, route_weights[:, :, None], 0.0), axis=1)
    earlier = jnp.tril(jnp.ones((tokens, tokens), jnp.bfloat16), -1)
    before = jnp.dot(earlier, member.astype(jnp.bfloat16), preferred_element_type=jnp.float32)
    position = jnp.where(member, before.astype(jnp.int32), -1)
    return position.T, weight.T


def per_device(
    teacher_in,
    routes,
    route_weights,
    expert_gate_up,
    expert_down,
    student_in,
    norm_gain,
    projector,
    second_moment,
):
    tokens_here, model_width = teacher_in.shape
    top_count = routes.shape[1]
    experts = lax.axis_size("expert")
    shares = lax.axis_size("fsdp")
    part = model_width // shares
    capacity = min(tokens_here, tokens_here * top_count * 9 // (8 * experts))
    position, weight = slot_maps(routes, route_weights, experts)
    onehot = position[:, None, :] == jnp.arange(capacity, dtype=jnp.int32)[None, :, None]
    select = onehot.astype(jnp.bfloat16)
    weighted = jnp.where(onehot, weight[:, None, :], 0.0)
    high = weighted.astype(jnp.bfloat16)
    low = (weighted - high.astype(jnp.float32)).astype(jnp.bfloat16)
    mine = lax.axis_index("fsdp") * part
    columns = lax.dynamic_slice_in_dim(teacher_in, mine, part, axis=1)
    buffer = jnp.einsum("est,tc->esc", select, columns, preferred_element_type=jnp.float32)
    buffer = buffer.astype(jnp.bfloat16)
    received = lax.all_to_all(buffer, "expert", split_axis=0, concat_axis=0, tiled=True)
    rows = lax.all_gather(received, "fsdp", axis=0)
    down_rows = lax.all_to_all(expert_down[0], "fsdp", split_axis=1, concat_axis=0, tiled=True)
    gate_up = expert_gate_up.reshape(shares, part, -1)
    gate_up_out = jnp.einsum("yesc,ycn->esn", rows, gate_up, preferred_element_type=jnp.float32)
    half = gate_up_out.shape[2] // 2
    hidden = (jax.nn.silu(gate_up_out[:, :, :half]) * gate_up_out[:, :, half:]).astype(jnp.bfloat16)
    hidden_all = lax.all_gather(hidden, "fsdp", axis=0)
    expert_out = jnp.einsum(
        "yesh,yhc->esc",
        hidden_all,
        down_rows.reshape(shares, half, part),
        preferred_element_type=jnp.float32,
    )
    returned = lax.all_to_all(
        expert_out.astype(jnp.bfloat16), "expert", split_axis=0, concat_axis=0, tiled=True
    )
    teacher = jnp.einsum(
        "est,esc->tc", high, returned, preferred_element_type=jnp.float32
    ) + jnp.einsum("est,esc->tc", low, returned, preferred_element_type=jnp.float32)
    student_wide = student_in.astype(jnp.float32)
    inv_rms = lax.rsqrt(jnp.mean(student_wide * student_wide, axis=1, keepdims=True) + 1e-06)
    normed = student_wide * inv_rms
    student_feat = (normed * norm_gain[None, :]).astype(jnp.bfloat16)
    residue = (
        jnp.dot(student_feat, projector, preferred_element_type=jnp.float32) - teacher
    ).astype(jnp.bfloat16)
    feat_part = jnp.einsum("tc,dc->td", residue, projector, preferred_element_type=jnp.float32)
    feat_grad = lax.psum(feat_part.astype(jnp.bfloat16), "fsdp").astype(jnp.float32)
    scaled = feat_grad * norm_gain[None, :]
    d_student = (
        inv_rms * (scaled - normed * jnp.mean(scaled * normed, axis=1, keepdims=True))
    ).astype(jnp.bfloat16)
    grad_block = lax.psum_scatter(
        jnp.einsum("tr,tc->rc", student_feat, residue, preferred_element_type=jnp.float32),
        "expert",
        scatter_dimension=0,
        tiled=True,
    )
    proj_step = grad_block / jnp.sqrt(
        beta_two * second_moment + (1.0 - beta_two) * grad_block * grad_block
    )
    return (d_student, proj_step)


def solution(mesh):
    placed = (
        P("expert", None),
        P("expert", None),
        P("expert", None),
        P("expert", None, None, "fsdp"),
        P("expert", "fsdp", None),
        P("expert", None),
        P(),
        P(None, "fsdp"),
        P("expert", "fsdp"),
    )
    return jax.shard_map(
        per_device,
        mesh=mesh,
        in_specs=placed,
        out_specs=(P("expert", None), P("expert", "fsdp")),
        check_vma=False,
    )
```

time: 963 us -> 569 us (0.59)
  waiting for transfers between devices: 764 us -> 350 us
  blocking collectives: 0 us -> 133 us
  local copies, waits for them, and re-layouts: 103 us -> 20.9 us
  other arithmetic: 37.7 us -> 7.36 us
  matrix products: 21.7 us -> 31.9 us
    all_to_all x2 -> x1, waiting for transfers between devices: 544 us -> 72.9 us  [per_device(): lax.all_to_all(expert_out.astype(jnp.bfloat16), 'expert', split_axis=0, c...]
    all_to_all x0 -> x2, blocking collectives: none -> 133 us  [the longest x1 84.8 us: per_device(): lax.all_to_all(buffer, 'expert', split_axis=0, concat_axis=0, tiled=True)]
    all_gather x0 -> x2, waiting for transfers between devices: none -> 84.6 us  [the longest x1 84.6 us: per_device(): rows = lax.all_gather(received, 'fsdp', axis=0)]
    reshape x3 -> x1, local copies, waits for them, and re-layouts: 42.1 us -> 7.6 us  [per_device(): gate_up = expert_gate_up.reshape(shares, part, -1)]
    gather x2 -> x0, local copies, waits for them, and re-layouts: 28 us -> none  [the longest x1 20 us: combine_rows(): flatten[targets]]
    reduce_scatter x1 -> x0, waiting for transfers between devices: 21.5 us -> none  [per_device(): lax.psum_scatter(combine_rows(returned, targets, route_weights).astype(jn...]
    another operation x3 -> x0, other arithmetic: 18.2 us -> none
    convert_element_type x1 -> x2, local copies, waits for them, and re-layouts: 20.4 us -> 4.42 us  [the longest x1 3.05 us: per_device(): expert_out.astype(jnp.bfloat16)]
  transfers between devices with their start and end apart: 5 -> 5, of which waited for: 5 -> 4; matrix products, arithmetic and copies ran while one was open for 1% -> 4% of each run, Pallas kernels for 0% -> 0%
where the time goes in v1:
time: 569 us; the launch traced here: 568 us
  waiting for transfers between devices  350 us (62%)
  blocking collectives  133 us (23%)
  matrix products  31.9 us (6%)
  local copies, waits for them, and re-layouts  20.9 us (4%)
  between operations  13.9 us (2%)
  starting transfers between devices  11 us (2%)
  other arithmetic  7.36 us (1%)
    reduce_scatter x1, waiting for transfers between devices, per_device(): lax.psum_scatter(jnp.einsum('tr,tc->rc', student_feat, residue, preferred...  153 us
    all_to_all x1, blocking collectives, per_device(): lax.all_to_all(buffer, 'expert', split_axis=0, concat_axis=0, tiled=True)  84.8 us
    all_gather x1, waiting for transfers between devices, per_device(): rows = lax.all_gather(received, 'fsdp', axis=0)  84.6 us
    all_to_all x1, waiting for transfers between devices, per_device(): lax.all_to_all(expert_out.astype(jnp.bfloat16), 'expert', split_axis=0, c...  72.9 us
    all_to_all x1, blocking collectives, per_device(): lax.all_to_all(expert_down[0], 'fsdp', split_axis=1, concat_axis=0, tiled...  48.3 us
    psum x1, waiting for transfers between devices, per_device(): lax.psum(feat_part.astype(jnp.bfloat16), 'fsdp').astype(jnp.float32)  38.8 us
  transfers between devices with their start and end apart: 5, of which 4 were waited for; matrix products, arithmetic and copies ran while one was open for 4% of the time, Pallas kernels for 0%

profile of v1, /device:TPU:8, one launch (start us, length us, event | category | flops | bytes accessed | tf_op | source)
XLA Modules:
  0.0 567.9 jit_solution(15985997728687819142)
XLA Ops:
  7.2 0.8 fusion.37
  8.0 0.2 fusion.19
  8.3 0.2 copy-done
  8.4 0.8 convolution_convert_fusion.1
  9.2 1.4 copy.35
  10.6 84.8 %all_to_all.26 = bf16[64,18,1024]{2,1,0:T(8,128)(2,1)S(1)} all-to-all(bf16[64,18,1024]{2,1,0:T(8,128)(2,1)S(1)} %copy.35), channel_id=1, replica_groups=mesh['expert'=64,'fsdp'=4] {'expert'}, dimensions={0} | all-to-all | bytes 4718592 | tf_op jit(solution)/shard_map/all_to_all | solution.py:47
  95.4 2.7 copy.36
  98.1 0.0 all-gather.7.cloned.1.call-start
  98.1 7.6 %reshape.34 = bf16[4,1024,512,1]{2,1,0,3:T(8,128)(2,1)} reshape(bf16[1,4096,2,256]{3,2,1,0:T(2,128)(2,1)} %param.12) | data formatting | bytes 8388608 | tf_op jit(solution)/shard_map/reshape | solution.py:50
  105.7 84.6 %all-gather.5.cloned.1.call-done = bf16[256,18,1024]{2,0,1:T(8,128)(2,1)} async-done(((bf16[64,18,1024]{2,0,1:T(8,128)(2,1)}), bf16[256,18,1024]{2,0,1:T(8,128)(2,1)}) %all-gather.5.cloned.1.call-update) | async-done | bytes 9437200 | tf_op jit(solution)/shard_map/all_gather | solution.py:48
  190.3 8.8 %convolution_bitcast_fusion = f32[64,18,512]{2,0,1:T(8,128)S(1)} fusion(bf16[4,64,18,1024]{3,1,0,2:T(8,128)(2,1)} %bitcast.37, bf16[4,1024,512,1]{2,1,0,3:T(8,128)(2,1)} %reshape.34), kind=kOutput, calls=%fused_computation.4 | convolution fusion | flops 4831838208 | bytes 15990784 | tf_op jit(solution)/shard_map/yesc,ycn->esn/dot_general | solution.py:51
  199.2 1.2 fusion.18
  200.4 0.6 copy-done.4
  201.0 2.4 copy.37
  203.4 3.0 copy.38
  206.4 48.3 %all_to_all.27 = bf16[256,4,1024]{2,0,1:T(8,128)(2,1)} all-to-all(bf16[256,4,1024]{2,0,1:T(8,128)(2,1)S(1)} %copy.38), channel_id=1, replica_groups=mesh['expert'=64,'fsdp'=4] {'fsdp'}, dimensions={1} | all-to-all | bytes 4194304 | tf_op jit(solution)/shard_map/all_to_all | solution.py:49
  254.7 4.9 bitcast_convert_fusion
  259.6 3.1 copy.39
  262.7 10.8 %all-to-all-start.2 = ((bf16[64,18,1024]{2,1,0:T(8,128)(2,1)}), bf16[64,18,1024]{2,1,0:T(8,128)(2,1)}, u32[]{:S(2)}, u32[]{:S(2)}) async-start(bf16[64,18,1024]{2,1,0:T(8,128)(2,1)} %copy.39), calls=%async_computation.2 | async-start | bytes 6291456 | tf_op jit(solution)/shard_map/all_to_all | solution.py:61
  273.6 0.2 fusion.25
  273.8 72.9 %all-to-all-done.2 = bf16[64,18,1024]{2,1,0:T(8,128)(2,1)} async-done(((bf16[64,18,1024]{2,1,0:T(8,128)(2,1)}), bf16[64,18,1024]{2,1,0:T(8,128)(2,1)}, u32[]{:S(2)}, u32[]{:S(2)}) %all-to-all-start.2) | async-done | bytes 2359328 | tf_op jit(solution)/shard_map/all_to_all | solution.py:61
  346.7 4.8 fusion.8
  351.5 4.7 fusion.14
  356.2 0.8 fusion.17
  357.1 2.3 convolution_convert_fusion
  359.4 0.0 reduce-scatter.2.cloned.1.call-start
  359.4 4.6 fusion.38
  364.1 38.8 %all-reduce.2.cloned.1.call-done = bf16[128,2048]{1,0:T(8,128)(2,1)} async-done(((bf16[128,2048]{1,0:T(8,128)(2,1)}), bf16[128,2048]{1,0:T(8,128)(2,1)}) %all-reduce.2.cloned.1.call-update) | async-done | bytes 524304 | tf_op jit(solution)/shard_map/psum | solution.py:75
  402.9 1.4 fusion.21
  404.3 2.2 fusion.24
  406.5 153.3 %reduce-scatter.2.cloned.1.call-done = f32[32,1024]{1,0:T(8,128)} async-done(((f32[2048,1024]{1,0:T(8,128)}), f32[32,1024]{1,0:T(8,128)}) %reduce-scatter.2.cloned.1.call-update) | async-done | bytes 131088 | tf_op jit(solution)/shard_map/reduce_scatter | solution.py:80
  559.8 1.6 fusion.43
  (27 shorter events, 0.2 us)
Async XLA Ops:
  7.2 1.2 copy-start
  7.2 183.2 %all-gather.5.cloned.1.call-start = ((), (), s32[]{:S(2)}) async-start(), calls=%async_computation.6 | async-start | bytes 11796480 | tf_op jit(solution)/shard_map/all_gather | solution.py:48
  98.1 156.6 %all-gather.7.cloned.1.call-start = ((), (), s32[]{:S(2)}) async-start(), calls=%async_computation.7 | async-start | bytes 2949120 | tf_op jit(solution)/shard_map/all_gather | solution.py:54
  199.2 1.8 copy-start.4
  262.7 10.9 %copy-start.7 = (s32[128,8]{0,1:T(8,128)S(1)}, s32[128,8]{0,1:T(8,128)}, u32[]{:S(2)}) copy-start(s32[128,8]{0,1:T(8,128)} %param.10) | copy-start | bytes 12292
  262.7 10.9 %copy-start.8 = (f32[128,8]{0,1:T(8,128)S(1)}, f32[128,8]{0,1:T(8,128)}, u32[]{:S(2)}) copy-start(f32[128,8]{0,1:T(8,128)} %param.11) | copy-start | bytes 12292
  262.7 10.9 %copy-start.3 = (bf16[128,2048]{1,0:T(8,128)(2,1)S(1)}, bf16[128,2048]{1,0:T(8,128)(2,1)}, u32[]{:S(2)}) copy-start(bf16[128,2048]{1,0:T(8,128)(2,1)} %param.14) | copy-start | bytes 1572868
  262.7 84.0 %all-to-all-start.2 = ((bf16[64,18,1024]{2,1,0:T(8,128)(2,1)}), bf16[64,18,1024]{2,1,0:T(8,128)(2,1)}, u32[]{:S(2)}, u32[]{:S(2)}) async-start(bf16[64,18,1024]{2,1,0:T(8,128)(2,1)} %copy.39), calls=%async_computation.2 | async-start | bytes 6291456 | tf_op jit(solution)/shard_map/all_to_all | solution.py:61
  273.5 129.4 %all-reduce.2.cloned.1.call-start = ((), (), s32[]{:S(2)}) async-start(), calls=%async_computation.4 | async-start | bytes 1048576 | tf_op jit(solution)/shard_map/psum | solution.py:75
  346.7 9.5 %copy-start.2 = (bf16[2048,1024]{1,0:T(8,128)(2,1)S(1)}, bf16[2048,1024]{1,0:T(8,128)(2,1)}, u32[]{:S(2)}) copy-start(bf16[2048,1024]{1,0:T(8,128)(2,1)} %param.16) | copy-start | bytes 12582916
  351.5 4.7 copy-start.5
  359.4 200.4 %reduce-scatter.2.cloned.1.call-start = ((), (), s32[]{:S(2)}) async-start(), calls=%async_computation.5 | async-start | bytes 8519680 | tf_op jit(solution)/shard_map/reduce_scatter | solution.py:80
  364.1 195.8 %copy-start.6 = (f32[32,1024]{1,0:T(8,128)S(1)}, f32[32,1024]{1,0:T(8,128)}, u32[]{:S(2)}) copy-start(f32[32,1024]{1,0:T(8,128)} %param.17) | copy-start | bytes 393220
  364.1 197.3 %copy-start.1 = (bf16[128,4096]{1,0:T(8,128)(2,1)S(1)}, bf16[128,4096]{1,0:T(8,128)(2,1)}, u32[]{:S(2)}) copy-start(bf16[128,4096]{1,0:T(8,128)(2,1)} %param.9) | copy-start | bytes 3145732
Sparse Core Ops, SparseCore 0:
  98.2 92.1 all-gather.4
  200.5 53.4 all-gather.6
  359.5 43.3 all-reduce.1
  407.0 152.7 reduce-scatter.1

commit v2 on v1

--- a/solution.py
+++ b/solution.py
@@ -1,9 +1,298 @@
 import jax
 import jax.numpy as jnp
 from jax import lax
+from jax.experimental import pallas as pl
+from jax.experimental.pallas import tpu as pltpu
 from jax.sharding import PartitionSpec as P
 
 beta_two = 0.95
+MESH = pl.DeviceIdType.MESH
+NX, NZ, NY = 4, 8, 4
+
+
+def remote(src, dst, send_sem, recv_sem, expert, share):
+    return pltpu.make_async_remote_copy(
+        src_ref=src,
+        dst_ref=dst,
+        send_sem=send_sem,
+        recv_sem=recv_sem,
+        device_id=(expert, share),
+        device_id_type=MESH,
+    )
+
+
+class Place:
+    def __init__(self):
+        expert = lax.axis_index("expert")
+        self.y = lax.axis_index("fsdp")
+        self.x = expert // (2 * NZ)
+        self.z = lax.rem(expert // 2, NZ)
+        self.k = lax.rem(expert, 2)
+
+    def at(self, dx=0, dz=0, dk=0):
+        x = lax.rem(self.x + dx, NX)
+        z = lax.rem(self.z + dz, NZ)
+        k = lax.rem(self.k + dk, 2)
+        return (x * NZ + z) * 2 + k
+
+    def member(self, dx=0, dk=0):
+        return lax.rem(self.x + dx, NX) * 2 + lax.rem(self.k + dk, 2)
+
+
+def meet(place):
+    barrier = pltpu.get_barrier_semaphore()
+    peers = [(place.at(dx=dx, dk=dk), place.y) for dx in range(NX) for dk in range(2) if dx or dk]
+    peers += [(place.at(dz=dz), place.y) for dz in range(1, NZ)]
+    peers += [(place.at(), lax.rem(place.y + dy, NY)) for dy in range(1, NY)]
+    for peer in peers:
+        pl.semaphore_signal(barrier, inc=1, device_id=peer, device_id_type=MESH)
+    pl.semaphore_wait(barrier, len(peers))
+
+
+def finish_kernel(
+    teacher_ref,
+    student_ref,
+    gain_ref,
+    projector_ref,
+    moment_ref,
+    d_ref,
+    step_ref,
+    feat_ref,
+    slab_ref,
+    slabs_ref,
+    residue_ref,
+    part_ref,
+    parts_ref,
+    d_own,
+    d_all,
+    grad_ref,
+    grads_ref,
+    own_grad,
+    slab_s,
+    slab_r,
+    res_s,
+    res_r,
+    fwd_s,
+    fwd_r,
+    part_s,
+    part_r,
+    d_s,
+    d_r,
+    grad_s,
+    grad_r,
+):
+    place = Place()
+    tokens, features = student_ref.shape
+    columns = projector_ref.shape[1]
+    rows = tokens // NY
+    mine = place.member()
+    meet(place)
+
+    def norm(wide):
+        inv = lax.rsqrt(jnp.mean(wide * wide, axis=1, keepdims=True) + 1e-06)
+        return inv, wide * inv
+
+    gain = gain_ref[...]
+    feat = norm(student_ref[...].astype(jnp.float32))[1] * gain
+    feat_ref[...] = feat.astype(jnp.bfloat16)
+    piece = features // (2 * NX * NZ)
+    for x in range(NX):
+        for z in range(NZ):
+            for k in range(2):
+                at = ((x * NZ + z) * 2 + k) * piece
+                if at % tokens == 0:
+                    turned = feat[:, at : at + tokens].T.astype(jnp.bfloat16)
+                slab_ref[x * 2 + k, z * piece : (z + 1) * piece, :] = turned[
+                    at % tokens : at % tokens + piece
+                ]
+
+    sends = []
+    slot = pl.ds(pl.multiple_of(mine * tokens, tokens), tokens)
+    i = 0
+    for dx in range(NX):
+        for dk in range(2):
+            if dx or dk:
+                to = place.at(dx=dx, dk=dk)
+                copy = remote(
+                    slab_ref.at[place.member(dx, dk)],
+                    slabs_ref.at[:, slot],
+                    slab_s.at[i],
+                    slab_r.at[i],
+                    to,
+                    place.y,
+                )
+                copy.start()
+                sends.append(copy)
+                i += 1
+    slabs_ref[:, slot] = slab_ref[mine]
+
+    width = 256
+
+    @pl.loop(0, columns // width)
+    def _(n):
+        cut = pl.ds(pl.multiple_of(n * width, width), width)
+        dense = jnp.dot(feat_ref[...], projector_ref[:, cut], preferred_element_type=jnp.float32)
+        residue_ref[slot, cut] = (dense - teacher_ref[:, cut]).astype(jnp.bfloat16)
+
+    def share(i, dx, dk):
+        copy = remote(
+            residue_ref.at[slot],
+            residue_ref.at[slot],
+            res_s.at[i],
+            res_r.at[i],
+            place.at(dx=dx, dk=dk),
+            place.y,
+        )
+        copy.start()
+        sends.append(copy)
+
+    share(2, 2, 0)
+    share(1, 1, 0)
+    share(3, 3, 0)
+    share(0, 0, 1)
+
+    @pl.loop(0, features // width)
+    def _(n):
+        cut = pl.ds(pl.multiple_of(n * width, width), width)
+        part_ref[:, cut] = lax.dot_general(
+            residue_ref[slot, :],
+            projector_ref[cut, :],
+            (((1,), (1,)), ((), ())),
+            preferred_element_type=jnp.float32,
+        ).astype(jnp.bfloat16)
+
+    for dy in (2, 1, 3):
+        to = lax.rem(place.y + dy, NY)
+        copy = remote(
+            part_ref.at[pl.ds(pl.multiple_of(to * rows, rows), rows)],
+            parts_ref.at[dy - 1],
+            part_s.at[dy - 1],
+            part_r.at[dy - 1],
+            place.at(),
+            to,
+        )
+        copy.start()
+        sends.append(copy)
+
+    def landed(ref, send_sem, recv_sem):
+        remote(ref, ref, send_sem, recv_sem, place.at(), place.y).wait_recv()
+
+    for dx in (1, 3, 2):
+        source = lax.rem(place.x + NX - dx, NX) * 2 + place.k
+        arrived = residue_ref.at[pl.ds(pl.multiple_of(source * tokens, tokens), tokens)]
+        landed(arrived, res_s.at[dx], res_r.at[dx])
+        copy = remote(
+            arrived, arrived, fwd_s.at[dx - 1], fwd_r.at[dx - 1], place.at(dk=1), place.y
+        )
+        copy.start()
+        sends.append(copy)
+
+    own_rows = pl.ds(pl.multiple_of(place.y * rows, rows), rows)
+    feat_grad = part_ref[own_rows, :].astype(jnp.float32)
+    for dy in range(1, NY):
+        landed(parts_ref.at[dy - 1], part_s.at[dy - 1], part_r.at[dy - 1])
+        feat_grad += parts_ref[dy - 1].astype(jnp.float32)
+    inv, normed = norm(student_ref[own_rows, :].astype(jnp.float32))
+    scaled = feat_grad * gain
+    d_own[...] = (
+        inv * (scaled - normed * jnp.mean(scaled * normed, axis=1, keepdims=True))
+    ).astype(jnp.bfloat16)
+    for dy in (2, 1, 3):
+        copy = remote(
+            d_own,
+            d_all.at[dy - 1],
+            d_s.at[dy - 1],
+            d_r.at[dy - 1],
+            place.at(),
+            lax.rem(place.y + dy, NY),
+        )
+        copy.start()
+        sends.append(copy)
+    d_ref[own_rows, :] = d_own[...]
+
+    i = 0
+    for dx in range(NX):
+        for dk in range(2):
+            if dx or dk:
+                source = place.member(NX - dx, dk)
+                at = pl.ds(pl.multiple_of(source * tokens, tokens), tokens)
+                landed(slabs_ref.at[:, at], slab_s.at[i], slab_r.at[i])
+                i += 1
+    other = 1 - place.k
+    partner = pl.ds(pl.multiple_of((place.x * 2 + other) * tokens, tokens), tokens)
+    landed(residue_ref.at[partner], res_s.at[0], res_r.at[0])
+    for dx in (1, 3, 2):
+        source = lax.rem(place.x + NX - dx, NX) * 2 + other
+        at = pl.ds(pl.multiple_of(source * tokens, tokens), tokens)
+        landed(residue_ref.at[at], fwd_s.at[dx - 1], fwd_r.at[dx - 1])
+
+    @pl.loop(0, columns // width)
+    def _(n):
+        cut = pl.ds(pl.multiple_of(n * width, width), width)
+        grad = jnp.dot(slabs_ref[...], residue_ref[:, cut], preferred_element_type=jnp.float32)
+        grad = grad.reshape(NZ, piece, width)
+        grad_ref[:, :, cut] = grad.astype(jnp.bfloat16)
+        own_grad[:, :, cut] = grad
+
+    for dz in (4, 3, 5, 2, 6, 1, 7):
+        copy = remote(
+            grad_ref.at[lax.rem(place.z + dz, NZ)],
+            grads_ref.at[dz - 1],
+            grad_s.at[dz - 1],
+            grad_r.at[dz - 1],
+            place.at(dz=dz),
+            place.y,
+        )
+        copy.start()
+        sends.append(copy)
+    for dy in range(1, NY):
+        source = lax.rem(place.y + NY - dy, NY)
+        landed(d_all.at[dy - 1], d_s.at[dy - 1], d_r.at[dy - 1])
+        d_ref[pl.ds(pl.multiple_of(source * rows, rows), rows), :] = d_all[dy - 1]
+    total = own_grad[place.z]
+    for dz in (1, 7, 2, 6, 3, 5, 4):
+        landed(grads_ref.at[dz - 1], grad_s.at[dz - 1], grad_r.at[dz - 1])
+        total += grads_ref[dz - 1].astype(jnp.float32)
+    step_ref[...] = total * lax.rsqrt(
+        beta_two * moment_ref[...] + (1.0 - beta_two) * total * total
+    )
+    for copy in sends:
+        copy.wait_send()
+
+
+def finish(teacher, student_in, norm_gain, projector, second_moment):
+    tokens, features = student_in.shape
+    columns = projector.shape[1]
+    rows = tokens // NY
+    piece = features // (2 * NX * NZ)
+    dma = pltpu.SemaphoreType.DMA
+    bf16, f32 = jnp.bfloat16, jnp.float32
+    return pl.pallas_call(
+        finish_kernel,
+        out_shape=(
+            jax.ShapeDtypeStruct((tokens, features), bf16),
+            jax.ShapeDtypeStruct(second_moment.shape, f32),
+        ),
+        in_specs=[pl.BlockSpec(memory_space=pltpu.VMEM)] * 5,
+        out_specs=[pl.BlockSpec(memory_space=pltpu.VMEM)] * 2,
+        scratch_shapes=[
+            pltpu.VMEM((tokens, features), bf16),
+            pltpu.VMEM((2 * NX, NZ * piece, tokens), bf16),
+            pltpu.VMEM((NZ * piece, 2 * NX * tokens), bf16),
+            pltpu.VMEM((2 * NX * tokens, columns), bf16),
+            pltpu.VMEM((tokens, features), bf16),
+            pltpu.VMEM((NY - 1, rows, features), bf16),
+            pltpu.VMEM((rows, features), bf16),
+            pltpu.VMEM((NY - 1, rows, features), bf16),
+            pltpu.VMEM((NZ, piece, columns), bf16),
+            pltpu.VMEM((NZ - 1, piece, columns), bf16),
+            pltpu.VMEM((NZ, piece, columns), f32),
+        ]
+        + [dma((n,)) for n in (7, 7, 4, 4, 3, 3, 3, 3, 3, 3, 7, 7)],
+        compiler_params=pltpu.CompilerParams(
+            collective_id=1, has_side_effects=True, vmem_limit_bytes=48 << 20
+        ),
+    )(teacher, student_in, norm_gain.reshape(1, -1), projector, second_moment)
 
 
 def slot_maps(routes, route_weights, experts):
@@ -64,29 +353,7 @@
     teacher = jnp.einsum(
         "est,esc->tc", high, returned, preferred_element_type=jnp.float32
     ) + jnp.einsum("est,esc->tc", low, returned, preferred_element_type=jnp.float32)
-    student_wide = student_in.astype(jnp.float32)
-    inv_rms = lax.rsqrt(jnp.mean(student_wide * student_wide, axis=1, keepdims=True) + 1e-06)
-    normed = student_wide * inv_rms
-    student_feat = (normed * norm_gain[None, :]).astype(jnp.bfloat16)
-    residue = (
-        jnp.dot(student_feat, projector, preferred_element_type=jnp.float32) - teacher
-    ).astype(jnp.bfloat16)
-    feat_part = jnp.einsum("tc,dc->td", residue, projector, preferred_element_type=jnp.float32)
-    feat_grad = lax.psum(feat_part.astype(jnp.bfloat16), "fsdp").astype(jnp.float32)
-    scaled = feat_grad * norm_gain[None, :]
-    d_student = (
-        inv_rms * (scaled - normed * jnp.mean(scaled * normed, axis=1, keepdims=True))
-    ).astype(jnp.bfloat16)
-    grad_block = lax.psum_scatter(
-        jnp.einsum("tr,tc->rc", student_feat, residue, preferred_element_type=jnp.float32),
-        "expert",
-        scatter_dimension=0,
-        tiled=True,
-    )
-    proj_step = grad_block / jnp.sqrt(
-        beta_two * second_moment + (1.0 - beta_two) * grad_block * grad_block
-    )
-    return (d_student, proj_step)
+    return finish(teacher, student_in, norm_gain, projector, second_moment)
 
 
 def solution(mesh):

time: 569 us -> 407 us (0.72)
  waiting for transfers between devices: 350 us -> 158 us
  Pallas kernels: 0 us -> 39.3 us
  matrix products: 31.9 us -> 24.3 us
    reduce_scatter x1 -> x0, waiting for transfers between devices: 153 us -> none  [per_device(): lax.psum_scatter(jnp.einsum('tr,tc->rc', student_feat, residue, preferred...]
    pallas_call x0 -> x1, Pallas kernels: none -> 39.3 us  [finish(): pl.pallas_call(finish_kernel, out_shape=(jax.ShapeDtypeStruct((tokens, fe...]
    psum x1 -> x0, waiting for transfers between devices: 38.8 us -> none  [per_device(): lax.psum(feat_part.astype(jnp.bfloat16), 'fsdp').astype(jnp.float32)]
    dot_general x3 -> x0, matrix products: 7.73 us -> none  [the longest x1 4.59 us: per_device(): jnp.einsum('tr,tc->rc', student_feat, residue, preferred_element_type=jnp...]
  transfers between devices with their start and end apart: 5 -> 3, of which waited for: 4 -> 2; matrix products, arithmetic and copies ran while one was open for 4% -> 3% of each run, Pallas kernels for 0% -> 0%
where the time goes in v2:
time: 407 us; the launch traced here: 404 us
  waiting for transfers between devices  158 us (39%)
  blocking collectives  133 us (33%)
  Pallas kernels  39.3 us (10%)
  matrix products  24.3 us (6%)
  local copies, waits for them, and re-layouts  22.4 us (6%)
  between operations  14.2 us (3%)
  starting transfers between devices  10.9 us (3%)
    all_to_all x1, blocking collectives, per_device(): lax.all_to_all(buffer, 'expert', split_axis=0, concat_axis=0, tiled=True)  84.8 us
    all_gather x1, waiting for transfers between devices, per_device(): rows = lax.all_gather(received, 'fsdp', axis=0)  84.6 us
    all_to_all x1, waiting for transfers between devices, per_device(): lax.all_to_all(expert_out.astype(jnp.bfloat16), 'expert', split_axis=0, c...  73.1 us
    all_to_all x1, blocking collectives, per_device(): lax.all_to_all(expert_down[0], 'fsdp', split_axis=1, concat_axis=0, tiled...  48.3 us
    pallas_call x1, Pallas kernels, finish(): pl.pallas_call(finish_kernel, out_shape=(jax.ShapeDtypeStruct((tokens, fe...  39.3 us
    all_to_all x1, starting transfers between devices, per_device(): lax.all_to_all(expert_out.astype(jnp.bfloat16), 'expert', split_axis=0, c...  10.8 us
    dot_general x1, matrix products, per_device(): jnp.einsum('yesc,ycn->esn', rows, gate_up, preferred_element_type=jnp.flo...  8.84 us
  transfers between devices with their start and end apart: 3, of which 2 were waited for; matrix products, arithmetic and copies ran while one was open for 3% of the time, Pallas kernels for 0%

profile of v2, /device:TPU:8, one launch (start us, length us, event | category | flops | bytes accessed | tf_op | source)
XLA Modules:
  0.0 404.0 jit_solution(10410015318175590126)
XLA Ops:
  7.2 0.0 copy-start
  7.2 0.0 all-gather.5.cloned.1.call-start
  7.2 0.8 fusion.27
  8.0 0.2 fusion.15
  8.2 0.2 copy-done
  8.4 0.8 convolution_convert_fusion
  9.2 1.4 copy.35
  10.6 84.8 %all_to_all.26 = bf16[64,18,1024]{2,1,0:T(8,128)(2,1)S(1)} all-to-all(bf16[64,18,1024]{2,1,0:T(8,128)(2,1)S(1)} %copy.35), channel_id=1, replica_groups=mesh['expert'=64,'fsdp'=4] {'expert'}, dimensions={0} | all-to-all | bytes 4718592 | tf_op jit(solution)/shard_map/all_to_all | solution.py:336
  95.4 2.7 copy.36
  98.1 0.0 all-gather.5.cloned.1.call-update
  98.1 0.0 all-gather.7.cloned.1.call-start
  98.1 7.6 %reshape.25 = bf16[4,1024,512,1]{2,1,0,3:T(8,128)(2,1)} reshape(bf16[1,4096,2,256]{3,2,1,0:T(2,128)(2,1)} %param.12) | data formatting | bytes 8388608 | tf_op jit(solution)/shard_map/reshape | solution.py:339
  105.8 84.6 %all-gather.5.cloned.1.call-done = bf16[256,18,1024]{2,0,1:T(8,128)(2,1)} async-done(((bf16[64,18,1024]{2,0,1:T(8,128)(2,1)}), bf16[256,18,1024]{2,0,1:T(8,128)(2,1)}) %all-gather.5.cloned.1.call-update) | async-done | bytes 9437200 | tf_op jit(solution)/shard_map/all_gather | solution.py:337
  190.4 8.8 %convolution_bitcast_fusion = f32[64,18,512]{2,0,1:T(8,128)S(1)} fusion(bf16[4,64,18,1024]{3,1,0,2:T(8,128)(2,1)} %bitcast.35, bf16[4,1024,512,1]{2,1,0,3:T(8,128)(2,1)} %reshape.25), kind=kOutput, calls=%fused_computation.3 | convolution fusion | flops 4831838208 | bytes 15990784 | tf_op jit(solution)/shard_map/yesc,ycn->esn/dot_general | solution.py:340
  199.2 0.0 copy-start.5
  199.2 1.2 fusion.14
  200.4 0.0 all-gather.7.cloned.1.call-update
  200.4 0.6 copy-done.5
  201.0 2.4 copy.37
  203.5 3.0 copy.38
  206.5 48.3 %all_to_all.27 = bf16[256,4,1024]{2,0,1:T(8,128)(2,1)} all-to-all(bf16[256,4,1024]{2,0,1:T(8,128)(2,1)S(1)} %copy.38), channel_id=1, replica_groups=mesh['expert'=64,'fsdp'=4] {'fsdp'}, dimensions={1} | all-to-all | bytes 4194304 | tf_op jit(solution)/shard_map/all_to_all | solution.py:338
  254.7 4.9 %bitcast_convert_fusion = bf16[64,18,1024]{2,0,1:T(8,128)(2,1)S(1)} fusion(bf16[4,64,18,256]{3,1,0,2:T(8,128)(2,1)} %bitcast.36, bf16[256,4,1024]{2,0,1:T(8,128)(2,1)} %all_to_all.27), kind=kOutput, calls=%fused_computation | convolution fusion | flops 2417098752 | bytes 6815744 | tf_op jit(solution)/shard_map/yesh,yhc->esc/dot_general | solution.py:344
  259.6 3.1 copy.39
  262.7 10.8 %all-to-all-start.2 = ((bf16[64,18,1024]{2,1,0:T(8,128)(2,1)}), bf16[64,18,1024]{2,1,0:T(8,128)(2,1)}, u32[]{:S(2)}, u32[]{:S(2)}) async-start(bf16[64,18,1024]{2,1,0:T(8,128)(2,1)} %copy.39), calls=%async_computation.2 | async-start | bytes 6291456 | tf_op jit(solution)/shard_map/all_to_all | solution.py:350
  273.6 73.1 %all-to-all-done.2 = bf16[64,18,1024]{2,1,0:T(8,128)(2,1)} async-done(((bf16[64,18,1024]{2,1,0:T(8,128)(2,1)}), bf16[64,18,1024]{2,1,0:T(8,128)(2,1)}, u32[]{:S(2)}, u32[]{:S(2)}) %all-to-all-start.2) | async-done | bytes 2359328 | tf_op jit(solution)/shard_map/all_to_all | solution.py:350
  346.7 4.8 %fusion.5 = f32[128,1024]{1,0:T(8,128)S(1)} fusion(bf16[64,18,1024]{2,1,0:T(8,128)(2,1)} %all-to-all-done.2, f32[64,128]{1,0:T(8,128)S(1)} %bitcast.33, s32[64,128]{1,0:T(8,128)S(1)} %fusion.15), kind=kOutput, calls=%fused_computation.8 | convolution fusion | flops 302284800 | bytes 2949120 | tf_op jit(solution)/shard_map/est,esc->tc/dot_general | solution.py:353
  351.5 0.0 copy-start.2
  351.5 0.0 copy-start.3
  351.6 4.7 %fusion.11.teacher_ref = f32[128,1024]{1,0:T(8,128)S(1)} fusion(f32[128,1024]{1,0:T(8,128)S(1)} %fusion.5, bf16[64,18,1024]{2,1,0:T(8,128)(2,1)} %all-to-all-done.2, f32[64,128]{1,0:T(8,128)S(1)} %bitcast.34, s32[64,128]{1,0:T(8,128)S(1)} %fusion.15), kind=kOutput, calls=%fused_computation.10 | convolution fusion | flops 303005696 | bytes 3473408 | tf_op jit(solution)/shard_map/est,esc->tc/dot_general | solution.py:355
  356.3 39.3 %shard_map.104 = (bf16[128,2048]{1,0:T(8,128)(2,1)S(1)}, f32[32,1024]{1,0:T(8,128)S(1)}) custom-call(f32[128,1024]{1,0:T(8,128)S(1)} %fusion.11.teacher_ref, bf16[128,2048]{1,0:T(8,128)(2,1)S(1)} %copy-done.2, f32[1,2048]{1,0:T(1,128)S(1)} %bitcast.31, bf16[2048,1024]{1,0:T(8,128)(2,1)S(1)} %copy-done.1, f32[32,1024]{1,0:T(8,128)S(1)} %copy-done.3), custom_call_target="tpu_custom_call" | custom-call | tf_op jit(solution)/shard_map/pallas_call | solution.py:270
  395.7 0.8 copy.56
  396.5 0.7 copy.57
  (13 shorter events, 0.1 us)
Async XLA Ops:
  7.2 1.2 copy-start
  7.2 183.2 %all-gather.5.cloned.1.call-start = ((), (), s32[]{:S(2)}) async-start(), calls=%async_computation.3 | async-start | bytes 11796480 | tf_op jit(solution)/shard_map/all_gather | solution.py:337
  98.1 156.6 %all-gather.7.cloned.1.call-start = ((), (), s32[]{:S(2)}) async-start(), calls=%async_computation.4 | async-start | bytes 2949120 | tf_op jit(solution)/shard_map/all_gather | solution.py:343
  199.2 1.8 copy-start.5
  262.7 10.8 %copy-start.6 = (s32[128,8]{0,1:T(8,128)S(1)}, s32[128,8]{0,1:T(8,128)}, u32[]{:S(2)}) copy-start(s32[128,8]{0,1:T(8,128)} %param.10) | copy-start | bytes 12292
  262.7 10.8 %copy-start.7 = (f32[128,8]{0,1:T(8,128)S(1)}, f32[128,8]{0,1:T(8,128)}, u32[]{:S(2)}) copy-start(f32[128,8]{0,1:T(8,128)} %param.11) | copy-start | bytes 12292
  262.7 84.0 %all-to-all-start.2 = ((bf16[64,18,1024]{2,1,0:T(8,128)(2,1)}), bf16[64,18,1024]{2,1,0:T(8,128)(2,1)}, u32[]{:S(2)}, u32[]{:S(2)}) async-start(bf16[64,18,1024]{2,1,0:T(8,128)(2,1)} %copy.39), calls=%async_computation.2 | async-start | bytes 6291456 | tf_op jit(solution)/shard_map/all_to_all | solution.py:350
  346.7 9.6 %copy-start.1 = (bf16[2048,1024]{1,0:T(8,128)(2,1)S(1)}, bf16[2048,1024]{1,0:T(8,128)(2,1)}, u32[]{:S(2)}) copy-start(bf16[2048,1024]{1,0:T(8,128)(2,1)} %projector_ref.1) | copy-start | bytes 12582916
  351.5 4.8 %copy-start.2 = (bf16[128,2048]{1,0:T(8,128)(2,1)S(1)}, bf16[128,2048]{1,0:T(8,128)(2,1)}, u32[]{:S(2)}) copy-start(bf16[128,2048]{1,0:T(8,128)(2,1)} %student_ref.1) | copy-start | bytes 1572868
  351.5 4.8 %copy-start.3 = (f32[32,1024]{1,0:T(8,128)S(1)}, f32[32,1024]{1,0:T(8,128)}, u32[]{:S(2)}) copy-start(f32[32,1024]{1,0:T(8,128)} %moment_ref.1) | copy-start | bytes 393220
  351.5 4.8 %copy-start.4 = (f32[2048]{0:T(1024)S(1)}, f32[2048]{0:T(1024)}, u32[]{:S(2)}) copy-start(f32[2048]{0:T(1024)} %param.15) | copy-start | bytes 24580
Sparse Core Ops, SparseCore 0:
  98.2 92.1 all-gather.4
  200.6 53.4 all-gather.6

commit v3 on v2

--- a/solution.py
+++ b/solution.py
@@ -47,6 +47,329 @@
     for peer in peers:
         pl.semaphore_signal(barrier, inc=1, device_id=peer, device_id_type=MESH)
     pl.semaphore_wait(barrier, len(peers))
+
+
+def experts_kernel(
+    teacher_in_ref,
+    meta_ref,
+    gate_up_ref,
+    down_ref,
+    out_ref,
+    tok_ref,
+    metas_ref,
+    select_ref,
+    spread_ref,
+    send_ref,
+    rows_ref,
+    hidden_ref,
+    down_all,
+    back_ref,
+    home_ref,
+    half_ref,
+    half_in,
+    total_ref,
+    third_ref,
+    third_in,
+    tok_s,
+    tok_r,
+    meta_s,
+    meta_r,
+    tokf_s,
+    tokf_r,
+    metaf_s,
+    metaf_r,
+    down_s,
+    down_r,
+    z_s,
+    z_r,
+    up_s,
+    up_r,
+    low_s,
+    low_r,
+    relay_s,
+    relay_r,
+    hid_s,
+    hid_r,
+    ret_s,
+    ret_r,
+    half_s,
+    half_r,
+    third_s,
+    third_r,
+):
+    place = Place()
+    tokens = teacher_in_ref.shape[0]
+    part = out_ref.shape[1]
+    units = down_ref.shape[0]
+    block = rows_ref.shape[2]
+    f32, bf16 = jnp.float32, jnp.bfloat16
+    y = place.y
+    mine = place.member()
+    meet(place)
+    sends = []
+
+    def send(*args):
+        copy = remote(*args)
+        copy.start()
+        sends.append(copy)
+
+    def landed(ref, send_sem, recv_sem):
+        remote(ref, ref, send_sem, recv_sem, place.at(), y).wait_recv()
+
+    def tok_slot(member):
+        return tok_ref.at[pl.ds(pl.multiple_of(member * tokens, tokens), tokens)]
+
+    def share_columns(share):
+        return pl.ds(pl.multiple_of(share * part, part), part)
+
+    own = teacher_in_ref.at[:, share_columns(y)]
+    for i, dx, dk in ((1, 1, 0), (3, 3, 0), (2, 2, 0), (0, 0, 1)):
+        to = place.at(dx=dx, dk=dk)
+        send(meta_ref, metas_ref.at[mine], meta_s.at[i], meta_r.at[i], to, y)
+        send(own, tok_slot(mine), tok_s.at[i], tok_r.at[i], to, y)
+    for dy in (2, 1, 3):
+        to = lax.rem(y + dy, NY)
+        send(
+            down_ref.at[:, share_columns(to)],
+            down_all.at[dy],
+            down_s.at[dy - 1],
+            down_r.at[dy - 1],
+            place.at(),
+            to,
+        )
+    tok_ref[pl.ds(pl.multiple_of(mine * tokens, tokens), tokens), :] = teacher_in_ref[
+        :, share_columns(y)
+    ]
+    metas_ref[mine] = meta_ref[...]
+    down_all[0] = down_ref[:, share_columns(y)]
+    for dx in (1, 3, 2):
+        source = place.member(NX - dx)
+        landed(metas_ref.at[source], meta_s.at[dx], meta_r.at[dx])
+        send(
+            metas_ref.at[source],
+            metas_ref.at[source],
+            metaf_s.at[dx - 1],
+            metaf_r.at[dx - 1],
+            place.at(dk=1),
+            y,
+        )
+        landed(tok_slot(source), tok_s.at[dx], tok_r.at[dx])
+        send(
+            tok_slot(source),
+            tok_slot(source),
+            tokf_s.at[dx - 1],
+            tokf_r.at[dx - 1],
+            place.at(dk=1),
+            y,
+        )
+    landed(metas_ref.at[place.member(0, 1)], meta_s.at[0], meta_r.at[0])
+    landed(tok_slot(place.member(0, 1)), tok_s.at[0], tok_r.at[0])
+    for dx in (1, 3, 2):
+        source = place.member(NX - dx, 1)
+        landed(metas_ref.at[source], metaf_s.at[dx - 1], metaf_r.at[dx - 1])
+        landed(tok_slot(source), tokf_s.at[dx - 1], tokf_r.at[dx - 1])
+
+    number = lax.broadcasted_iota(jnp.int32, (block, tokens), 0).astype(f32)
+    order = (0, 1, 7, 2, 6, 3, 5, 4)
+
+    for dz in order:
+        expert = place.at(dz=dz)
+        for o in range(2 * NX):
+            code = metas_ref[o, 0, pl.ds(expert, 1), :]
+            select_ref[:, o * tokens : (o + 1) * tokens] = jnp.where(
+                number == code, 1.0, 0.0
+            ).astype(bf16)
+        picked = jnp.dot(select_ref[...], tok_ref[...], preferred_element_type=f32).astype(bf16)
+        if dz == 0:
+            rows_ref[0, 0] = picked
+        else:
+            send_ref[dz - 1] = picked
+            send(
+                send_ref.at[dz - 1],
+                rows_ref.at[0, dz],
+                z_s.at[dz - 1],
+                z_r.at[dz - 1],
+                expert,
+                y,
+            )
+
+    after, ahead = lax.rem(y + 1, NY), lax.rem(y + NY - 1, NY)
+
+    def pass_rows(j):
+        dz = order[j]
+        if dz:
+            landed(rows_ref.at[0, dz], z_s.at[dz - 1], z_r.at[dz - 1])
+        send(rows_ref.at[0, dz], rows_ref.at[1, dz], up_s.at[dz], up_r.at[dz], place.at(), after)
+        send(rows_ref.at[0, dz], rows_ref.at[3, dz], low_s.at[dz], low_r.at[dz], place.at(), ahead)
+
+    def relay_rows(j):
+        dz = order[j]
+        landed(rows_ref.at[1, dz], up_s.at[dz], up_r.at[dz])
+        landed(rows_ref.at[3, dz], low_s.at[dz], low_r.at[dz])
+        source, to = (1, after) if j % 2 == 0 else (3, ahead)
+        send(
+            rows_ref.at[source, dz],
+            rows_ref.at[2, dz],
+            relay_s.at[dz],
+            relay_r.at[dz],
+            place.at(),
+            to,
+        )
+
+    def first_product(j):
+        dz = order[j]
+        landed(rows_ref.at[2, dz], relay_s.at[dz], relay_r.at[dz])
+        out = jnp.zeros((block, 2 * units), f32)
+        for ry in range(NY):
+            share = lax.rem(y + NY - ry, NY)
+            out += jnp.dot(
+                rows_ref[ry, dz],
+                gate_up_ref[share_columns(share), :],
+                preferred_element_type=f32,
+            )
+        gate, up = out[:, :units], out[:, units:]
+        hidden_ref[0, dz] = (gate / (1.0 + jnp.exp(-gate)) * up).astype(bf16)
+        for dy in (2, 1, 3):
+            send(
+                hidden_ref.at[0, dz],
+                hidden_ref.at[dy, dz],
+                hid_s.at[dy - 1, dz],
+                hid_r.at[dy - 1, dz],
+                place.at(),
+                lax.rem(y + dy, NY),
+            )
+
+    def second_product(j):
+        dz = order[j]
+        for dy in range(1, NY):
+            landed(hidden_ref.at[dy, dz], hid_s.at[dy - 1, dz], hid_r.at[dy - 1, dz])
+        out = jnp.zeros((block, part), f32)
+        for ry in range(NY):
+            out += jnp.dot(hidden_ref[ry, dz], down_all[ry], preferred_element_type=f32)
+        if dz == 0:
+            home_ref[0:block, :] = out.astype(bf16)
+        else:
+            back_ref[dz - 1] = out.astype(bf16)
+            send(
+                back_ref.at[dz - 1],
+                home_ref.at[dz * block : (dz + 1) * block],
+                ret_s.at[dz - 1],
+                ret_r.at[dz - 1],
+                place.at(dz=NZ - dz),
+                y,
+            )
+
+    def weigh():
+        for dk in (1, 0):
+            for dx in range(NX):
+                o = place.member(dx, dk)
+                pieces = []
+                for dz in range(NZ):
+                    expert = pl.ds(place.at(dz=dz), 1)
+                    pieces.append(
+                        jnp.where(number == metas_ref[o, 0, expert, :], metas_ref[o, 1, expert, :], 0.0)
+                    )
+                at = ((1 - dk) * NX + dx) * tokens
+                spread_ref[at : at + tokens, :] = jnp.concatenate(pieces, axis=0).T.astype(bf16)
+
+    steps = len(order)
+    pass_rows(0)
+    weigh()
+    for dy in range(1, NY):
+        landed(down_all.at[dy], down_s.at[dy - 1], down_r.at[dy - 1])
+    for j in range(1, steps + 4):
+        if j < steps:
+            pass_rows(j)
+        if 0 <= j - 1 < steps:
+            relay_rows(j - 1)
+        if 0 <= j - 2 < steps:
+            first_product(j - 2)
+        if 0 <= j - 4 < steps:
+            second_product(j - 4)
+
+    for dz in order[1:]:
+        landed(home_ref.at[dz * block : (dz + 1) * block], ret_s.at[dz - 1], ret_r.at[dz - 1])
+    width = 256
+    count = NX * tokens
+
+    @pl.loop(0, part // width)
+    def _(n):
+        cut = pl.ds(pl.multiple_of(n * width, width), width)
+        half_ref[:, cut] = jnp.dot(
+            spread_ref[:count, :], home_ref[:, cut], preferred_element_type=f32
+        ).astype(bf16)
+
+    send(half_ref, half_in, half_s.at[0], half_r.at[0], place.at(dk=1), y)
+
+    @pl.loop(0, part // width)
+    def _(n):
+        cut = pl.ds(pl.multiple_of(n * width, width), width)
+        total_ref[:, cut] = jnp.dot(
+            spread_ref[count:, :], home_ref[:, cut], preferred_element_type=f32
+        )
+
+    landed(half_in, half_s.at[0], half_r.at[0])
+    for dx in (2, 1, 3):
+        at = slice(dx * tokens, (dx + 1) * tokens)
+        third_ref[dx - 1] = (total_ref[at, :] + half_in[at, :].astype(f32)).astype(bf16)
+        send(
+            third_ref.at[dx - 1],
+            third_in.at[dx - 1],
+            third_s.at[dx - 1],
+            third_r.at[dx - 1],
+            place.at(dx=dx),
+            y,
+        )
+    teacher = total_ref[:tokens, :] + half_in[:tokens, :].astype(f32)
+    for dx in (1, 3, 2):
+        landed(third_in.at[dx - 1], third_s.at[dx - 1], third_r.at[dx - 1])
+        teacher += third_in[dx - 1].astype(f32)
+    out_ref[...] = teacher
+    for copy in sends:
+        copy.wait_send()
+
+
+def experts_output(teacher_in, meta, gate_up, down, capacity):
+    tokens, width = teacher_in.shape
+    part = width // NY
+    units = down.shape[0]
+    oct_size = 2 * NX
+    block = oct_size * capacity
+    dma = pltpu.SemaphoreType.DMA
+    bf16, f32 = jnp.bfloat16, jnp.float32
+    return pl.pallas_call(
+        experts_kernel,
+        out_shape=jax.ShapeDtypeStruct((tokens, part), f32),
+        in_specs=[pl.BlockSpec(memory_space=pltpu.VMEM)] * 4,
+        out_specs=pl.BlockSpec(memory_space=pltpu.VMEM),
+        scratch_shapes=[
+            pltpu.VMEM((oct_size * tokens, part), bf16),
+            pltpu.VMEM((oct_size,) + meta.shape, f32),
+            pltpu.VMEM((block, oct_size * tokens), bf16),
+            pltpu.VMEM((oct_size * tokens, NZ * block), bf16),
+            pltpu.VMEM((NZ - 1, block, part), bf16),
+            pltpu.VMEM((NY, NZ, block, part), bf16),
+            pltpu.VMEM((NY, NZ, block, units), bf16),
+            pltpu.VMEM((NY, units, part), bf16),
+            pltpu.VMEM((NZ - 1, block, part), bf16),
+            pltpu.VMEM((NZ * block, part), bf16),
+            pltpu.VMEM((NX * tokens, part), bf16),
+            pltpu.VMEM((NX * tokens, part), bf16),
+            pltpu.VMEM((NX * tokens, part), f32),
+            pltpu.VMEM((NX - 1, tokens, part), bf16),
+            pltpu.VMEM((NX - 1, tokens, part), bf16),
+        ]
+        + [
+            dma(n)
+            for n in (
+                [(4,)] * 4 + [(3,)] * 4 + [(3,)] * 2 + [(7,)] * 2 + [(8,)] * 6
+                + [(3, 8)] * 2 + [(7,)] * 2 + [(1,)] * 2 + [(3,)] * 2
+            )
+        ],
+        compiler_params=pltpu.CompilerParams(
+            collective_id=0, has_side_effects=True, vmem_limit_bytes=58 << 20
+        ),
+    )(teacher_in, meta, gate_up, down)
 
 
 def finish_kernel(
@@ -317,42 +640,15 @@
     projector,
     second_moment,
 ):
-    tokens_here, model_width = teacher_in.shape
+    tokens_here = teacher_in.shape[0]
     top_count = routes.shape[1]
     experts = lax.axis_size("expert")
-    shares = lax.axis_size("fsdp")
-    part = model_width // shares
     capacity = min(tokens_here, tokens_here * top_count * 9 // (8 * experts))
     position, weight = slot_maps(routes, route_weights, experts)
-    onehot = position[:, None, :] == jnp.arange(capacity, dtype=jnp.int32)[None, :, None]
-    select = onehot.astype(jnp.bfloat16)
-    weighted = jnp.where(onehot, weight[:, None, :], 0.0)
-    high = weighted.astype(jnp.bfloat16)
-    low = (weighted - high.astype(jnp.float32)).astype(jnp.bfloat16)
-    mine = lax.axis_index("fsdp") * part
-    columns = lax.dynamic_slice_in_dim(teacher_in, mine, part, axis=1)
-    buffer = jnp.einsum("est,tc->esc", select, columns, preferred_element_type=jnp.float32)
-    buffer = buffer.astype(jnp.bfloat16)
-    received = lax.all_to_all(buffer, "expert", split_axis=0, concat_axis=0, tiled=True)
-    rows = lax.all_gather(received, "fsdp", axis=0)
-    down_rows = lax.all_to_all(expert_down[0], "fsdp", split_axis=1, concat_axis=0, tiled=True)
-    gate_up = expert_gate_up.reshape(shares, part, -1)
-    gate_up_out = jnp.einsum("yesc,ycn->esn", rows, gate_up, preferred_element_type=jnp.float32)
-    half = gate_up_out.shape[2] // 2
-    hidden = (jax.nn.silu(gate_up_out[:, :, :half]) * gate_up_out[:, :, half:]).astype(jnp.bfloat16)
-    hidden_all = lax.all_gather(hidden, "fsdp", axis=0)
-    expert_out = jnp.einsum(
-        "yesh,yhc->esc",
-        hidden_all,
-        down_rows.reshape(shares, half, part),
-        preferred_element_type=jnp.float32,
-    )
-    returned = lax.all_to_all(
-        expert_out.astype(jnp.bfloat16), "expert", split_axis=0, concat_axis=0, tiled=True
-    )
-    teacher = jnp.einsum(
-        "est,esc->tc", high, returned, preferred_element_type=jnp.float32
-    ) + jnp.einsum("est,esc->tc", low, returned, preferred_element_type=jnp.float32)
+    code = jnp.where(position >= 0, position + Place().member() * capacity, -1)
+    meta = jnp.stack([code.astype(jnp.float32), weight])
+    gate_up = expert_gate_up.reshape(expert_gate_up.shape[1], -1)
+    teacher = experts_output(teacher_in, meta, gate_up, expert_down[0], capacity)
     return finish(teacher, student_in, norm_gain, projector, second_moment)
 
 

time: 407 us -> 250 us (0.61)
  Pallas kernels: 39.3 us -> 235 us
  waiting for transfers between devices: 158 us -> 0 us
  blocking collectives: 133 us -> 0 us
  matrix products: 24.3 us -> 0.23 us
  local copies, waits for them, and re-layouts: 22.4 us -> 7.36 us
  between operations: 14.2 us -> 0.74 us
  starting transfers between devices: 10.9 us -> 0 us
    pallas_call x0 -> x1, Pallas kernels: none -> 194 us  [experts_output(): pl.pallas_call(experts_kernel, out_shape=jax.ShapeDtypeStruct((tokens, pa...]
    all_to_all x2 -> x0, blocking collectives: 133 us -> none  [the longest x1 84.8 us: per_device(): lax.all_to_all(buffer, 'expert', split_axis=0, concat_axis=0, tiled=True)]
    all_gather x2 -> x0, waiting for transfers between devices: 84.6 us -> none  [the longest x1 84.6 us: per_device(): rows = lax.all_gather(received, 'fsdp', axis=0)]
    all_to_all x1 -> x0, waiting for transfers between devices: 73.1 us -> none  [per_device(): lax.all_to_all(expert_out.astype(jnp.bfloat16), 'expert', split_axis=0, c...]
    dot_general x5 -> x0, matrix products: 24.1 us -> none  [the longest x1 8.84 us: per_device(): jnp.einsum('yesc,ycn->esn', rows, gate_up, preferred_element_type=jnp.flo...]
    all_to_all x1 -> x0, starting transfers between devices: 10.8 us -> none  [per_device(): lax.all_to_all(expert_out.astype(jnp.bfloat16), 'expert', split_axis=0, c...]
    reshape x1 -> x0, local copies, waits for them, and re-layouts: 7.62 us -> none  [per_device(): gate_up = expert_gate_up.reshape(shares, part, -1)]
    all_to_all x2 -> x0, local copies, waits for them, and re-layouts: 5.69 us -> none  [the longest x1 2.99 us: per_device(): lax.all_to_all(expert_down[0], 'fsdp', split_axis=1, concat_axis=0, tiled...]
  transfers between devices with their start and end apart: 3 -> 0, of which waited for: 2 -> 0; matrix products, arithmetic and copies ran while one was open for 3% -> 0% of each run, Pallas kernels for 0% -> 0%
where the time goes in v3:
time: 250 us; the launch traced here: 245 us
  Pallas kernels  235 us (94%)
  local copies, waits for them, and re-layouts  7.36 us (3%)
    pallas_call x1, Pallas kernels, experts_output(): pl.pallas_call(experts_kernel, out_shape=jax.ShapeDtypeStruct((tokens, pa...  194 us
    pallas_call x1, Pallas kernels, finish(): pl.pallas_call(finish_kernel, out_shape=(jax.ShapeDtypeStruct((tokens, fe...  41.4 us
    unnamed x13, local copies, waits for them, and re-layouts  7.36 us

profile of v3, /device:TPU:8, one launch (start us, length us, event | category | flops | bytes accessed | tf_op | source)
XLA Modules:
  0.0 245.4 jit_solution(11204906651988161269)
XLA Ops:
  0.7 0.7 fusion.1
  1.4 0.2 convert_bitcast_fusion
  1.6 0.7 select_reduce_fusion
  2.4 0.6 pad_maximum_fusion.meta_ref
  3.0 4.9 %copy.13 = bf16[512,8,2,256]{3,1,2,0:T(8,128)(2,1)} copy(bf16[512,8,2,256]{3,2,1,0:T(2,128)(2,1)} %bitcast.17) | data formatting | bytes 8388608
  7.9 0.0 copy-start
  7.9 0.0 copy-start.2
  7.9 0.0 copy-start.3
  7.9 0.0 copy-start.4
  7.9 193.6 %shard_map.104.teacher_ref = f32[128,1024]{1,0:T(8,128)} custom-call(bf16[128,4096]{1,0:T(8,128)(2,1)} %teacher_in_ref.1, f32[2,64,128]{2,1,0:T(8,128)} %pad_maximum_fusion.meta_ref, bf16[4096,512]{1,0:T(8,128)(2,1)} %bitcast.16, bf16[256,4096]{1,0:T(8,128)(2,1)} %bitcast.18), custom_call_target="tpu_custom_call" | custom-call | tf_op jit(solution)/shard_map/pallas_call | solution.py:340
  201.4 0.0 copy-done
  201.5 0.0 copy-done.2
  201.5 0.0 copy-done.3
  201.5 0.0 copy-done.4
  201.5 0.0 copy-start.1
  201.5 1.0 copy-done.1
  202.5 41.4 %shard_map.105 = (bf16[128,2048]{1,0:T(8,128)(2,1)S(1)}, f32[32,1024]{1,0:T(8,128)S(1)}) custom-call(f32[128,1024]{1,0:T(8,128)S(1)} %copy-done.1, bf16[128,2048]{1,0:T(8,128)(2,1)S(1)} %copy-done.2, f32[1,2048]{1,0:T(1,128)S(1)} %bitcast.15, bf16[2048,1024]{1,0:T(8,128)(2,1)S(1)} %copy-done, f32[32,1024]{1,0:T(8,128)S(1)} %copy-done.3), custom_call_target="tpu_custom_call" | custom-call | tf_op jit(solution)/shard_map/pallas_call | solution.py:593
  244.0 0.8 copy.16
  244.8 0.7 copy.17
  (1 shorter events, 0.0 us)
Async XLA Ops:
  7.9 193.6 %copy-start = (bf16[2048,1024]{1,0:T(8,128)(2,1)S(1)}, bf16[2048,1024]{1,0:T(8,128)(2,1)}, u32[]{:S(2)}) copy-start(bf16[2048,1024]{1,0:T(8,128)(2,1)} %projector_ref.1) | copy-start | bytes 12582916
  7.9 193.6 %copy-start.2 = (bf16[128,2048]{1,0:T(8,128)(2,1)S(1)}, bf16[128,2048]{1,0:T(8,128)(2,1)}, u32[]{:S(2)}) copy-start(bf16[128,2048]{1,0:T(8,128)(2,1)} %student_ref.1) | copy-start | bytes 1572868
  7.9 193.6 %copy-start.3 = (f32[32,1024]{1,0:T(8,128)S(1)}, f32[32,1024]{1,0:T(8,128)}, u32[]{:S(2)}) copy-start(f32[32,1024]{1,0:T(8,128)} %moment_ref.1) | copy-start | bytes 393220
  7.9 193.6 %copy-start.4 = (f32[2048]{0:T(1024)S(1)}, f32[2048]{0:T(1024)}, u32[]{:S(2)}) copy-start(f32[2048]{0:T(1024)} %param.15) | copy-start | bytes 24580
  201.5 1.0 copy-start.1

commit v4 on v1

v4 whole, which is shorter than its diff:
```python
import functools
import types

import jax
import jax.numpy as jnp
from jax import lax
from jax.experimental import pallas as pl
from jax.experimental.pallas import tpu as pltpu
from jax.sharding import PartitionSpec as P

beta_two = 0.95
MESH = pl.DeviceIdType.MESH
NX, NZ, NY = 4, 8, 4
OCT = 2 * NX
WIDTH = 256
ORDER = (0, 4, 3, 5, 2, 6, 1, 7)


def remote(src, dst, send_sem, recv_sem, expert, share):
    return pltpu.make_async_remote_copy(
        src_ref=src,
        dst_ref=dst,
        send_sem=send_sem,
        recv_sem=recv_sem,
        device_id=(expert, share),
        device_id_type=MESH,
    )


class Place:
    def __init__(self):
        expert = lax.axis_index("expert")
        self.y = lax.axis_index("fsdp")
        self.x = expert // (2 * NZ)
        self.z = lax.rem(expert // 2, NZ)
        self.k = lax.rem(expert, 2)

    def at(self, dx=0, dz=0, dk=0):
        x = lax.rem(self.x + dx, NX)
        z = lax.rem(self.z + dz, NZ)
        k = lax.rem(self.k + dk, 2)
        return (x * NZ + z) * 2 + k

    def member(self, dx=0, dk=0):
        return lax.rem(self.x + dx, NX) * 2 + lax.rem(self.k + dk, 2)


def meet(place):
    barrier = pltpu.get_barrier_semaphore()
    peers = [(place.at(dx=dx, dk=dk), place.y) for dx in range(NX) for dk in range(2) if dx or dk]
    peers += [(place.at(dz=dz), place.y) for dz in range(1, NZ)]
    peers += [(place.at(), lax.rem(place.y + dy, NY)) for dy in range(1, NY)]
    for peer in peers:
        pl.semaphore_signal(barrier, inc=1, device_id=peer, device_id_type=MESH)
    pl.semaphore_wait(barrier, len(peers))


def cut_of(n, width):
    return slice(n * width, (n + 1) * width)


def part_of(index, size):
    return pl.ds(pl.multiple_of(index * size, size), size)


def norm(wide):
    inv = lax.rsqrt(jnp.mean(wide * wide, axis=1, keepdims=True) + 1e-06)
    return inv, wide * inv


def dot(a, b):
    return jnp.dot(a, b, preferred_element_type=jnp.float32)


class Gather:
    def __init__(self, place, send, landed, ref, tokens, width, sems):
        self.place, self.send, self.landed = place, send, landed
        self.ref, self.tokens, self.width = ref, tokens, width
        self.near_s, self.near_r, self.pass_s, self.pass_r = sems

    def slot(self, c, dx=0, dk=0):
        at = part_of(self.place.member(dx, dk), self.tokens)
        return self.ref.at[at, cut_of(c, self.width)]

    def start(self, c, own=None):
        own = self.slot(c) if own is None else own
        for i, dx, dk in ((1, 1, 0), (3, NX - 1, 0), (0, 0, 1)):
            to = self.place.at(dx=dx, dk=dk)
            self.send(own, self.slot(c), self.near_s.at[i, c], self.near_r.at[i, c], to, self.place.y)

    def onward(self, c, i):
        arrived = self.slot(c, NX - i)
        to = self.place.at(dk=1)
        self.send(arrived, arrived, self.pass_s.at[i - 1, c], self.pass_r.at[i - 1, c], to, self.place.y)

    def relay(self, c):
        for i in (1, 3):
            self.landed(self.slot(c, NX - i), self.near_s.at[i, c], self.near_r.at[i, c])
            if i == (1 if c % 2 == 0 else 3):
                arrived = self.slot(c, NX - i)
                to = self.place.at(dx=i)
                self.send(arrived, arrived, self.near_s.at[2, c], self.near_r.at[2, c], to, self.place.y)
            self.onward(c, i)

    def far(self, c):
        self.landed(self.slot(c, 2), self.near_s.at[2, c], self.near_r.at[2, c])
        self.onward(c, 2)

    def finish(self, c):
        self.landed(self.slot(c, 0, 1), self.near_s.at[0, c], self.near_r.at[0, c])
        for i in (1, 3, 2):
            self.landed(self.slot(c, NX - i, 1), self.pass_s.at[i - 1, c], self.pass_r.at[i - 1, c])


def layer_kernel(names, *refs):
    r = types.SimpleNamespace(**dict(zip(names, refs)))
    place = Place()
    y = place.y
    tokens, features = r.student.shape
    part = r.projector.shape[1]
    units = r.down.shape[0]
    block = r.rows.shape[2]
    piece = r.step.shape[0]
    share_rows = tokens // NY
    chunks = part // WIDTH
    f32, bf16 = jnp.float32, jnp.bfloat16
    mine = place.member()
    steps = len(ORDER)
    after, ahead = lax.rem(y + 1, NY), lax.rem(y + NY - 1, NY)

    own_tokens = r.tok.at[part_of(mine, tokens)]
    loads = [
        pltpu.make_async_copy(r.teacher_in.at[:, part_of(y, part)], own_tokens, r.load.at[0]),
        pltpu.make_async_copy(r.projector, r.proj, r.load.at[1]),
        pltpu.make_async_copy(r.gate_up, r.gates, r.load.at[2]),
        pltpu.make_async_copy(r.down.at[:, part_of(y, part)], r.down_all.at[0], r.load.at[3]),
    ]
    for load in loads:
        load.start()
    meet(place)
    sends = []

    def send(*args):
        copy = remote(*args)
        copy.start()
        sends.append(copy)

    def landed(ref, send_sem, recv_sem):
        remote(ref, ref, send_sem, recv_sem, place.at(), y).wait_recv()

    members = [(dx, dk) for dx in range(NX) for dk in range(2) if dx or dk]

    half = part // 2
    tok = Gather(
        place, send, landed, r.tok, tokens, half, (r.tok_s, r.tok_r, r.tokf_s, r.tokf_r)
    )
    for i, (dx, dk) in enumerate(members):
        to = place.at(dx=dx, dk=dk)
        send(r.meta.at[place.member(dx, dk)], r.metas.at[mine], r.meta_s.at[i], r.meta_r.at[i], to, y)
    loads[0].wait()
    for c in range(2):
        tok.start(c)
    for dy in (2, 1, 3):
        to = lax.rem(y + dy, NY)
        send(
            r.down.at[:, part_of(to, part)],
            r.down_all.at[dy],
            r.down_s.at[dy - 1],
            r.down_r.at[dy - 1],
            place.at(),
            to,
        )
    r.metas[mine] = r.meta[mine]
    for i, (dx, dk) in enumerate(members):
        landed(r.metas.at[place.member(NX - dx, dk)], r.meta_s.at[i], r.meta_r.at[i])
    for c in range(2):
        tok.relay(c)

    number = lax.broadcasted_iota(jnp.int32, (block, tokens), 0).astype(f32)
    for dk in (1, 0):
        for dx in range(NX):
            o = place.member(dx, dk)
            pieces = []
            for dz in range(NZ):
                at = pl.ds(lax.rem(place.z + dz, NZ), 1)
                pieces.append(jnp.where(number == r.metas[o, 0, at, :], r.metas[o, 1, at, :], 0.0))
            at = ((1 - dk) * NX + dx) * tokens
            r.spread[at : at + tokens, :] = jnp.concatenate(pieces, axis=0).T.astype(bf16)
    for c in range(2):
        tok.far(c)

    gain = r.gain[...]
    feat = norm(r.student[...].astype(f32))[1] * gain
    r.feat[...] = feat.astype(bf16)
    for x in range(NX):
        for z in range(NZ):
            for k in range(2):
                at = ((x * NZ + z) * 2 + k) * piece
                if at % tokens == 0:
                    turned = feat[:, at : at + tokens].T.astype(bf16)
                r.slab[x * 2 + k, z * piece : (z + 1) * piece, :] = turned[
                    at % tokens : at % tokens + piece
                ]
    for c in range(2):
        tok.finish(c)

    for dz in ORDER:
        at = pl.ds(lax.rem(place.z + dz, NZ), 1)
        for o in range(OCT):
            r.select[:, cut_of(o, tokens)] = jnp.where(number == r.metas[o, 0, at, :], 1.0, 0.0).astype(
                bf16
            )
        picked = dot(r.select[...], r.tok[...]).astype(bf16)
        if dz == 0:
            r.rows[0, 0] = picked
            send(r.rows.at[0, 0], r.rows.at[1, 0], r.up_s.at[0], r.up_r.at[0], place.at(), after)
            send(r.rows.at[0, 0], r.rows.at[3, 0], r.low_s.at[0], r.low_r.at[0], place.at(), ahead)
        else:
            r.out[dz - 1] = picked
            send(
                r.out.at[dz - 1], r.rows.at[0, dz], r.z_s.at[dz - 1], r.z_r.at[dz - 1], place.at(dz=dz), y
            )

    slot = part_of(mine, tokens)
    for i, (dx, dk) in enumerate(members):
        send(
            r.slab.at[place.member(dx, dk)],
            r.slabs.at[:, slot],
            r.slab_s.at[i],
            r.slab_r.at[i],
            place.at(dx=dx, dk=dk),
            y,
        )
    r.slabs[:, slot] = r.slab[mine]
    loads[1].wait()
    loads[2].wait()
    loads[3].wait()

    def pass_rows(j):
        dz = ORDER[j]
        landed(r.rows.at[0, dz], r.z_s.at[dz - 1], r.z_r.at[dz - 1])
        send(r.rows.at[0, dz], r.rows.at[1, dz], r.up_s.at[dz], r.up_r.at[dz], place.at(), after)
        send(r.rows.at[0, dz], r.rows.at[3, dz], r.low_s.at[dz], r.low_r.at[dz], place.at(), ahead)

    def relay_rows(j):
        dz = ORDER[j]
        landed(r.rows.at[1, dz], r.up_s.at[dz], r.up_r.at[dz])
        landed(r.rows.at[3, dz], r.low_s.at[dz], r.low_r.at[dz])
        source, to = (1, after) if j % 2 == 0 else (3, ahead)
        send(r.rows.at[source, dz], r.rows.at[2, dz], r.far_s.at[dz], r.far_r.at[dz], place.at(), to)

    def first_product(j):
        dz = ORDER[j]
        landed(r.rows.at[2, dz], r.far_s.at[dz], r.far_r.at[dz])
        out = jnp.zeros((block, 2 * units), f32)
        for ry in range(NY):
            share = lax.rem(y + NY - ry, NY)
            out += dot(r.rows[ry, dz], r.gates[part_of(share, part), :])
        gate, up = out[:, :units], out[:, units:]
        r.hidden[0, dz] = (gate / (1.0 + jnp.exp(-gate)) * up).astype(bf16)
        for dy, to in ((1, after), (3, ahead)):
            send(
                r.hidden.at[0, dz], r.hidden.at[dy, dz], r.hid_s.at[dy, dz], r.hid_r.at[dy, dz], place.at(), to
            )

    def relay_hidden(j):
        dz = ORDER[j]
        for dy in (1, 3):
            landed(r.hidden.at[dy, dz], r.hid_s.at[dy, dz], r.hid_r.at[dy, dz])
        source, to = (1, after) if j % 2 == 0 else (3, ahead)
        send(r.hidden.at[source, dz], r.hidden.at[2, dz], r.hid_s.at[2, dz], r.hid_r.at[2, dz], place.at(), to)

    def second_product(j):
        dz = ORDER[j]
        landed(r.hidden.at[2, dz], r.hid_s.at[2, dz], r.hid_r.at[2, dz])
        out = jnp.zeros((block, part), f32)
        for ry in range(NY):
            out += dot(r.hidden[ry, dz], r.down_all[ry])
        if dz == 0:
            r.home[0:block, :] = out.astype(bf16)
        else:
            r.back[dz - 1] = out.astype(bf16)
            send(
                r.back.at[dz - 1],
                r.home.at[cut_of(dz, block)],
                r.ret_s.at[dz - 1],
                r.ret_r.at[dz - 1],
                place.at(dz=NZ - dz),
                y,
            )

    for j in range(1, steps + 4):
        if j < steps:
            pass_rows(j)
        if 0 <= j - 1 < steps:
            relay_rows(j - 1)
        if j == 1:
            for n in range(chunks):
                r.dense[:, cut_of(n, WIDTH)] = dot(r.feat[...], r.proj[:, cut_of(n, WIDTH)])
        if 0 <= j - 2 < steps:
            first_product(j - 2)
        if 0 <= j - 3 < steps:
            relay_hidden(j - 3)
        if j == 4:
            for dy in range(1, NY):
                landed(r.down_all.at[dy], r.down_s.at[dy - 1], r.down_r.at[dy - 1])
        if 0 <= j - 4 < steps:
            second_product(j - 4)

    for dz in ORDER[1:]:
        landed(r.home.at[cut_of(dz, block)], r.ret_s.at[dz - 1], r.ret_r.at[dz - 1])

    count = NX * tokens
    for n in range(chunks):
        r.half[n] = dot(r.spread[:count, :], r.home[:, cut_of(n, WIDTH)]).astype(bf16)
        send(r.half.at[n], r.half_in.at[n], r.half_s.at[n], r.half_r.at[n], place.at(dk=1), y)
    for n in range(chunks):
        r.total[n] = dot(r.spread[count:, :], r.home[:, cut_of(n, WIDTH)])
        landed(r.half_in.at[n], r.half_s.at[n], r.half_r.at[n])
        for dx in (2, 1, 3):
            at = cut_of(dx, tokens)
            r.third[dx - 1, n] = (r.total[n, at, :] + r.half_in[n, at, :].astype(f32)).astype(bf16)
            send(
                r.third.at[dx - 1, n],
                r.third_in.at[dx - 1, n],
                r.third_s.at[dx - 1, n],
                r.third_r.at[dx - 1, n],
                place.at(dx=dx),
                y,
            )

    res = Gather(
        place, send, landed, r.residue, tokens, WIDTH, (r.res_s, r.res_r, r.resf_s, r.resf_r)
    )
    for n in range(chunks + 2):
        if n < chunks:
            teacher = r.total[n, :tokens, :] + r.half_in[n, :tokens, :].astype(f32)
            for dx in (1, 3, 2):
                landed(r.third_in.at[dx - 1, n], r.third_s.at[dx - 1, n], r.third_r.at[dx - 1, n])
                teacher += r.third_in[dx - 1, n].astype(f32)
            cut = cut_of(n, WIDTH)
            r.residue[slot, cut] = (r.dense[:, cut] - teacher).astype(bf16)
            res.start(n)
        if 0 <= n - 1 < chunks:
            res.relay(n - 1)
        if 0 <= n - 2 < chunks:
            res.far(n - 2)

    for n in range(features // WIDTH):
        r.part[:, cut_of(n, WIDTH)] = lax.dot_general(
            r.residue[slot, :],
            r.proj[cut_of(n, WIDTH), :],
            (((1,), (1,)), ((), ())),
            preferred_element_type=f32,
        ).astype(bf16)
    for dy in (2, 1, 3):
        to = lax.rem(y + dy, NY)
        send(
            r.part.at[part_of(to, share_rows)],
            r.parts.at[dy - 1],
            r.part_s.at[dy - 1],
            r.part_r.at[dy - 1],
            place.at(),
            to,
        )

    for i, (dx, dk) in enumerate(members):
        at = part_of(place.member(NX - dx, dk), tokens)
        landed(r.slabs.at[:, at], r.slab_s.at[i], r.slab_r.at[i])
    for n in range(chunks):
        res.finish(n)
        grad = dot(r.slabs[...], r.residue[:, cut_of(n, WIDTH)]).reshape(NZ, piece, WIDTH)
        r.grad[n] = grad.astype(bf16)
        r.own_grad[n] = grad
        for dz in (4, 3, 5, 2, 6, 1, 7):
            send(
                r.grad.at[n, lax.rem(place.z + dz, NZ)],
                r.grads.at[dz - 1, n],
                r.grad_s.at[dz - 1, n],
                r.grad_r.at[dz - 1, n],
                place.at(dz=dz),
                y,
            )

    own_rows = part_of(y, share_rows)
    feat_grad = r.part[own_rows, :].astype(f32)
    for dy in range(1, NY):
        landed(r.parts.at[dy - 1], r.part_s.at[dy - 1], r.part_r.at[dy - 1])
        feat_grad += r.parts[dy - 1].astype(f32)
    inv, normed = norm(r.student[own_rows, :].astype(f32))
    scaled = feat_grad * gain
    r.d_own[...] = (
        inv * (scaled - normed * jnp.mean(scaled * normed, axis=1, keepdims=True))
    ).astype(bf16)
    for dy in (2, 1, 3):
        to = lax.rem(y + dy, NY)
        send(r.d_own, r.d_all.at[dy - 1], r.d_s.at[dy - 1], r.d_r.at[dy - 1], place.at(), to)
    r.d[own_rows, :] = r.d_own[...]

    for n in range(chunks):
        total = r.own_grad[n, place.z]
        for dz in (1, 7, 2, 6, 3, 5, 4):
            landed(r.grads.at[dz - 1, n], r.grad_s.at[dz - 1, n], r.grad_r.at[dz - 1, n])
            total += r.grads[dz - 1, n].astype(f32)
        cut = cut_of(n, WIDTH)
        r.step[:, cut] = total * lax.rsqrt(
            beta_two * r.moment[:, cut] + (1.0 - beta_two) * total * total
        )
    for dy in range(1, NY):
        landed(r.d_all.at[dy - 1], r.d_s.at[dy - 1], r.d_r.at[dy - 1])
        r.d[part_of(lax.rem(y + NY - dy, NY), share_rows), :] = r.d_all[dy - 1]
    for copy in sends:
        copy.wait_send()


def layer(teacher_in, meta, gate_up, down, student_in, norm_gain, projector, second_moment, capacity):
    tokens, features = student_in.shape
    part = projector.shape[1]
    units = down.shape[0]
    block = OCT * capacity
    piece = second_moment.shape[0]
    share_rows = tokens // NY
    chunks = part // WIDTH
    bf16, f32 = jnp.bfloat16, jnp.float32
    vmem, anywhere = pl.BlockSpec(memory_space=pltpu.VMEM), pl.BlockSpec(memory_space=pl.ANY)
    inputs = dict(
        teacher_in=(teacher_in, anywhere),
        meta=(meta, vmem),
        gate_up=(gate_up, anywhere),
        down=(down, anywhere),
        student=(student_in, vmem),
        gain=(norm_gain.reshape(1, -1), vmem),
        projector=(projector, anywhere),
        moment=(second_moment, vmem),
    )
    outputs = dict(
        d=jax.ShapeDtypeStruct((tokens, features), bf16),
        step=jax.ShapeDtypeStruct(second_moment.shape, f32),
    )
    buffers = dict(
        proj=(projector.shape, bf16),
        gates=(gate_up.shape, bf16),
        tok=((OCT * tokens, part), bf16),
        metas=(meta.shape, f32),
        select=((block, OCT * tokens), bf16),
        spread=((OCT * tokens, NZ * block), bf16),
        out=((NZ - 1, block, part), bf16),
        rows=((NY, NZ, block, part), bf16),
        hidden=((NY, NZ, block, units), bf16),
        down_all=((NY, units, part), bf16),
        back=((NZ - 1, block, part), bf16),
        home=((NZ * block, part), bf16),
        half=((chunks, NX * tokens, WIDTH), bf16),
        half_in=((chunks, NX * tokens, WIDTH), bf16),
        total=((chunks, NX * tokens, WIDTH), f32),
        third=((NX - 1, chunks, tokens, WIDTH), bf16),
        third_in=((NX - 1, chunks, tokens, WIDTH), bf16),
        feat=((tokens, features), bf16),
        dense=((tokens, part), f32),
        slab=((OCT, NZ * piece, tokens), bf16),
        slabs=((NZ * piece, OCT * tokens), bf16),
        residue=((OCT * tokens, part), bf16),
        part=((tokens, features), bf16),
        parts=((NY - 1, share_rows, features), bf16),
        d_own=((share_rows, features), bf16),
        d_all=((NY - 1, share_rows, features), bf16),
        grad=((chunks, NZ, piece, WIDTH), bf16),
        grads=((NZ - 1, chunks, piece, WIDTH), bf16),
        own_grad=((chunks, NZ, piece, WIDTH), f32),
    )
    flights = dict(
        meta=(OCT - 1,),
        tok=(4, 2),
        tokf=(3, 2),
        down=(NY - 1,),
        z=(NZ - 1,),
        up=(NZ,),
        low=(NZ,),
        far=(NZ,),
        hid=(NY, NZ),
        ret=(NZ - 1,),
        half=(chunks,),
        third=(NX - 1, chunks),
        slab=(OCT - 1,),
        res=(4, chunks),
        resf=(3, chunks),
        part=(NY - 1,),
        d=(NY - 1,),
        grad=(NZ - 1, chunks),
    )
    dma = pltpu.SemaphoreType.DMA
    pairs = {f"{name}_{end}": dma(shape) for name, shape in flights.items() for end in "sr"}
    names = (*inputs, *outputs, *buffers, *pairs, "load")
    return pl.pallas_call(
        functools.partial(layer_kernel, names),
        out_shape=tuple(outputs.values()),
        in_specs=[spec for _, spec in inputs.values()],
        out_specs=[vmem] * len(outputs),
        scratch_shapes=[pltpu.VMEM(*b) for b in buffers.values()] + [*pairs.values(), dma((4,))],
        compiler_params=pltpu.CompilerParams(
            collective_id=0, has_side_effects=True, vmem_limit_bytes=60 << 20
        ),
    )(*(value for value, _ in inputs.values()))


def slot_maps(routes, route_weights, experts):
    tokens = routes.shape[0]
    named = routes[:, :, None] == jnp.arange(experts, dtype=jnp.int32)[None, None, :]
    member = jnp.any(named, axis=1)
    weight = jnp.sum(jnp.where(named, route_weights[:, :, None], 0.0), axis=1)
    earlier = jnp.tril(jnp.ones((tokens, tokens), jnp.bfloat16), -1)
    before = jnp.dot(earlier, member.astype(jnp.bfloat16), preferred_element_type=jnp.float32)
    position = jnp.where(member, before.astype(jnp.int32), -1)
    return position.T, weight.T


def per_device(
    teacher_in,
    routes,
    route_weights,
    expert_gate_up,
    expert_down,
    student_in,
    norm_gain,
    projector,
    second_moment,
):
    tokens_here = teacher_in.shape[0]
    top_count = routes.shape[1]
    experts = lax.axis_size("expert")
    capacity = min(tokens_here, tokens_here * top_count * 9 // (8 * experts))
    position, weight = slot_maps(routes, route_weights, experts)
    code = jnp.where(position >= 0, position + Place().member() * capacity, -1)
    meta = jnp.stack([code.astype(jnp.float32), weight])
    meta = meta.reshape(2, NX, NZ, 2, tokens_here).transpose(1, 3, 0, 2, 4)
    meta = meta.reshape(OCT, 2, NZ, tokens_here)
    gate_up = expert_gate_up.reshape(expert_gate_up.shape[1], -1)
    return layer(
        teacher_in,
        meta,
        gate_up,
        expert_down[0],
        student_in,
        norm_gain,
        projector,
        second_moment,
        capacity,
    )


def solution(mesh):
    placed = (
        P("expert", None),
        P("expert", None),
        P("expert", None),
        P("expert", None, None, "fsdp"),
        P("expert", "fsdp", None),
        P("expert", None),
        P(),
        P(None, "fsdp"),
        P("expert", "fsdp"),
    )
    return jax.shard_map(
        per_device,
        mesh=mesh,
        in_specs=placed,
        out_specs=(P("expert", None), P("expert", "fsdp")),
        check_vma=False,
    )
```

time: 569 us -> 225 us (0.40)
  waiting for transfers between devices: 350 us -> 0 us
  Pallas kernels: 0 us -> 213 us
  blocking collectives: 133 us -> 0 us
  matrix products: 31.9 us -> 0.23 us
  between operations: 13.9 us -> 0.7 us
  local copies, waits for them, and re-layouts: 20.9 us -> 8.93 us
  starting transfers between devices: 11 us -> 0 us
  other arithmetic: 7.36 us -> 1.5 us
    pallas_call x0 -> x1, Pallas kernels: none -> 213 us  [layer(): pl.pallas_call(functools.partial(layer_kernel, names), out_shape=tuple(ou...]
    reduce_scatter x1 -> x0, waiting for transfers between devices: 153 us -> none  [per_device(): lax.psum_scatter(jnp.einsum('tr,tc->rc', student_feat, residue, preferred...]
    all_to_all x2 -> x0, blocking collectives: 133 us -> none  [the longest x1 84.8 us: per_device(): lax.all_to_all(buffer, 'expert', split_axis=0, concat_axis=0, tiled=True)]
    all_gather x2 -> x0, waiting for transfers between devices: 84.6 us -> none  [the longest x1 84.6 us: per_device(): rows = lax.all_gather(received, 'fsdp', axis=0)]
    all_to_all x1 -> x0, waiting for transfers between devices: 72.9 us -> none  [per_device(): lax.all_to_all(expert_out.astype(jnp.bfloat16), 'expert', split_axis=0, c...]
    psum x1 -> x0, waiting for transfers between devices: 38.8 us -> none  [per_device(): lax.psum(feat_part.astype(jnp.bfloat16), 'fsdp').astype(jnp.float32)]
    dot_general x8 -> x0, matrix products: 31.7 us -> none  [the longest x1 8.84 us: per_device(): jnp.einsum('yesc,ycn->esn', rows, gate_up, preferred_element_type=jnp.flo...]
    all_to_all x1 -> x0, starting transfers between devices: 10.8 us -> none  [per_device(): lax.all_to_all(expert_out.astype(jnp.bfloat16), 'expert', split_axis=0, c...]
  transfers between devices with their start and end apart: 5 -> 0, of which waited for: 4 -> 0; matrix products, arithmetic and copies ran while one was open for 4% -> 0% of each run, Pallas kernels for 0% -> 0%
where the time goes in v4:
time: 225 us; the launch traced here: 224 us
  Pallas kernels  213 us (95%)
  local copies, waits for them, and re-layouts  8.93 us (4%)
    pallas_call x1, Pallas kernels, layer(): pl.pallas_call(functools.partial(layer_kernel, names), out_shape=tuple(ou...  213 us
    unnamed x3, local copies, waits for them, and re-layouts  8.29 us

profile of v4, /device:TPU:8, one launch (start us, length us, event | category | flops | bytes accessed | tf_op | source)
XLA Modules:
  0.0 224.1 jit_solution(18198907454018207808)
XLA Ops:
  0.7 0.7 fusion.1
  1.4 0.2 select_convert_fusion
  1.6 0.7 select_reduce_fusion
  2.4 0.6 copy.17
  3.1 4.8 %copy.18 = bf16[512,8,2,256]{3,1,2,0:T(8,128)(2,1)} copy(bf16[512,8,2,256]{3,2,1,0:T(2,128)(2,1)} %bitcast.18) | data formatting | bytes 8388608
  7.9 212.8 %shard_map.104 = (bf16[128,2048]{1,0:T(8,128)(2,1)}, f32[32,1024]{1,0:T(8,128)}) custom-call(bf16[128,4096]{1,0:T(8,128)(2,1)} %refs_0_.1, f32[8,2,8,128]{3,2,1,0:T(8,128)} %bitcast.20, bf16[4096,512]{1,0:T(8,128)(2,1)} %bitcast.17, bf16[256,4096]{1,0:T(8,128)(2,1)} %bitcast.19, bf16[128,2048]{1,0:T(8,128)(2,1)} %refs_4_.1, f32[1,2048]{1,0:T(1,128)} %bitcast.23, ...), custom_call_target="tpu_custom_call" | custom-call | tf_op jit(solution)/shard_map/pallas_call | solution.py:494
  220.7 1.9 copy.21
  222.6 1.6 copy.22
  (2 shorter events, 0.0 us)

commit v5 on v4

--- a/solution.py
+++ b/solution.py
@@ -13,7 +13,7 @@
 NX, NZ, NY = 4, 8, 4
 OCT = 2 * NX
 WIDTH = 256
-ORDER = (0, 4, 3, 5, 2, 6, 1, 7)
+ORDER = (0, 1, 2, 6, 4, 5, 3, 7)
 
 
 def remote(src, dst, send_sem, recv_sem, expert, share):
@@ -128,12 +128,18 @@
     steps = len(ORDER)
     after, ahead = lax.rem(y + 1, NY), lax.rem(y + NY - 1, NY)
 
-    own_tokens = r.tok.at[part_of(mine, tokens)]
+    capacity = block // NZ
+    far_share = lax.rem(y + 2, NY)
     loads = [
-        pltpu.make_async_copy(r.teacher_in.at[:, part_of(y, part)], own_tokens, r.load.at[0]),
-        pltpu.make_async_copy(r.projector, r.proj, r.load.at[1]),
-        pltpu.make_async_copy(r.gate_up, r.gates, r.load.at[2]),
-        pltpu.make_async_copy(r.down.at[:, part_of(y, part)], r.down_all.at[0], r.load.at[3]),
+        pltpu.make_async_copy(
+            r.teacher_in.at[:, part_of(y, part)], r.tok.at[0, cut_of(0, tokens)], r.load.at[0]
+        ),
+        pltpu.make_async_copy(
+            r.teacher_in.at[:, part_of(far_share, part)], r.tok.at[1, cut_of(0, tokens)], r.load.at[1]
+        ),
+        pltpu.make_async_copy(r.projector, r.proj, r.load.at[2]),
+        pltpu.make_async_copy(r.gate_up, r.gates, r.load.at[3]),
+        pltpu.make_async_copy(r.down.at[:, part_of(y, part)], r.down_all.at[0], r.load.at[4]),
     ]
     for load in loads:
         load.start()
@@ -151,15 +157,47 @@
     members = [(dx, dk) for dx in range(NX) for dk in range(2) if dx or dk]
 
     half = part // 2
-    tok = Gather(
-        place, send, landed, r.tok, tokens, half, (r.tok_s, r.tok_r, r.tokf_s, r.tokf_r)
-    )
-    for i, (dx, dk) in enumerate(members):
-        to = place.at(dx=dx, dk=dk)
-        send(r.meta.at[place.member(dx, dk)], r.metas.at[mine], r.meta_s.at[i], r.meta_r.at[i], to, y)
+
+    def ring_slot(q, way, hops, c):
+        d = hops if way == 0 else (NZ - hops) % NZ
+        return r.tok.at[q, cut_of(d, tokens), cut_of(c, half)]
+
+    def ring_send(q, way, hops, c):
+        i = way * NZ + hops * 2 + c
+        send(
+            ring_slot(q, way, hops, c),
+            ring_slot(q, way, hops + 1, c),
+            r.tok_s.at[q, i],
+            r.tok_r.at[q, i],
+            place.at(dz=1 if way == 0 else NZ - 1),
+            y,
+        )
+
+    def ring_start(q):
+        for c in range(2):
+            for way in range(2):
+                ring_send(q, way, 0, c)
+
+    def ring_step(q, hops):
+        for c in range(2):
+            for way in range(2):
+                if hops < NZ // 2 or c == way:
+                    i = way * NZ + (hops - 1) * 2 + c
+                    landed(ring_slot(q, way, hops, c), r.tok_s.at[q, i], r.tok_r.at[q, i])
+                if hops < NZ // 2 - 1 or (hops == NZ // 2 - 1 and c == way):
+                    ring_send(q, way, hops, c)
+
+    for dz in range(1, NZ):
+        send(
+            r.meta.at[lax.rem(place.z + dz, NZ)],
+            r.metas.at[dz],
+            r.meta_s.at[dz - 1],
+            r.meta_r.at[dz - 1],
+            place.at(dz=dz),
+            y,
+        )
     loads[0].wait()
-    for c in range(2):
-        tok.start(c)
+    ring_start(0)
     for dy in (2, 1, 3):
         to = lax.rem(y + dy, NY)
         send(
@@ -170,28 +208,14 @@
             place.at(),
             to,
         )
-    r.metas[mine] = r.meta[mine]
-    for i, (dx, dk) in enumerate(members):
-        landed(r.metas.at[place.member(NX - dx, dk)], r.meta_s.at[i], r.meta_r.at[i])
-    for c in range(2):
-        tok.relay(c)
-
-    number = lax.broadcasted_iota(jnp.int32, (block, tokens), 0).astype(f32)
-    for dk in (1, 0):
-        for dx in range(NX):
-            o = place.member(dx, dk)
-            pieces = []
-            for dz in range(NZ):
-                at = pl.ds(lax.rem(place.z + dz, NZ), 1)
-                pieces.append(jnp.where(number == r.metas[o, 0, at, :], r.metas[o, 1, at, :], 0.0))
-            at = ((1 - dk) * NX + dx) * tokens
-            r.spread[at : at + tokens, :] = jnp.concatenate(pieces, axis=0).T.astype(bf16)
-    for c in range(2):
-        tok.far(c)
+    r.metas[0] = r.meta[place.z]
+    ring_step(0, 1)
 
     gain = r.gain[...]
     feat = norm(r.student[...].astype(f32))[1] * gain
     r.feat[...] = feat.astype(bf16)
+    ring_step(0, 2)
+
     for x in range(NX):
         for z in range(NZ):
             for k in range(2):
@@ -201,25 +225,55 @@
                 r.slab[x * 2 + k, z * piece : (z + 1) * piece, :] = turned[
                     at % tokens : at % tokens + piece
                 ]
-    for c in range(2):
-        tok.finish(c)
-
-    for dz in ORDER:
-        at = pl.ds(lax.rem(place.z + dz, NZ), 1)
-        for o in range(OCT):
-            r.select[:, cut_of(o, tokens)] = jnp.where(number == r.metas[o, 0, at, :], 1.0, 0.0).astype(
-                bf16
+    ring_step(0, 3)
+    loads[1].wait()
+    ring_start(1)
+    for dz in range(1, NZ):
+        landed(r.metas.at[dz], r.meta_s.at[dz - 1], r.meta_r.at[dz - 1])
+    ring_step(0, 4)
+
+    number = lax.broadcasted_iota(jnp.int32, (block, tokens), 0).astype(f32)
+
+    def expert_at(i):
+        return pl.ds(place.member(i // 2, i % 2), 1)
+
+    def select_rows(q, i):
+        for d in range(NZ):
+            code = r.metas[d, 0, expert_at(i), :] + float(d * capacity)
+            r.select[:, cut_of(d, tokens)] = jnp.where(number == code, 1.0, 0.0).astype(bf16)
+        picked = dot(r.select[...], r.tok[q]).astype(bf16)
+        if i == 0:
+            r.rows[2 * q, 0] = picked
+        else:
+            r.out[q, i - 1] = picked
+            send(
+                r.out.at[q, i - 1],
+                r.rows.at[2 * q, i],
+                r.x_s.at[q, i - 1],
+                r.x_r.at[q, i - 1],
+                place.at(dx=i // 2, dk=i % 2),
+                y,
             )
-        picked = dot(r.select[...], r.tok[...]).astype(bf16)
-        if dz == 0:
-            r.rows[0, 0] = picked
-            send(r.rows.at[0, 0], r.rows.at[1, 0], r.up_s.at[0], r.up_r.at[0], place.at(), after)
-            send(r.rows.at[0, 0], r.rows.at[3, 0], r.low_s.at[0], r.low_r.at[0], place.at(), ahead)
-        else:
-            r.out[dz - 1] = picked
-            send(
-                r.out.at[dz - 1], r.rows.at[0, dz], r.z_s.at[dz - 1], r.z_r.at[dz - 1], place.at(dz=dz), y
-            )
+
+    def pass_rows(j):
+        i = ORDER[j]
+        if i:
+            landed(r.rows.at[0, i], r.x_s.at[0, i - 1], r.x_r.at[0, i - 1])
+        send(r.rows.at[0, i], r.rows.at[1, i], r.up_s.at[i], r.up_r.at[i], place.at(), after)
+        send(r.rows.at[0, i], r.rows.at[3, i], r.low_s.at[i], r.low_r.at[i], place.at(), ahead)
+
+    for j in range(steps):
+        select_rows(0, ORDER[j])
+        if j == 0:
+            pass_rows(0)
+        if j % 2 == 1:
+            ring_step(1, (j + 1) // 2)
+        if j >= 3:
+            pass_rows(j - 2)
+    for j in range(steps):
+        select_rows(1, ORDER[j])
+        if j < 2:
+            pass_rows(steps - 2 + j)
 
     slot = part_of(mine, tokens)
     for i, (dx, dk) in enumerate(members):
@@ -232,120 +286,122 @@
             y,
         )
     r.slabs[:, slot] = r.slab[mine]
-    loads[1].wait()
-    loads[2].wait()
-    loads[3].wait()
-
-    def pass_rows(j):
-        dz = ORDER[j]
-        landed(r.rows.at[0, dz], r.z_s.at[dz - 1], r.z_r.at[dz - 1])
-        send(r.rows.at[0, dz], r.rows.at[1, dz], r.up_s.at[dz], r.up_r.at[dz], place.at(), after)
-        send(r.rows.at[0, dz], r.rows.at[3, dz], r.low_s.at[dz], r.low_r.at[dz], place.at(), ahead)
-
-    def relay_rows(j):
-        dz = ORDER[j]
-        landed(r.rows.at[1, dz], r.up_s.at[dz], r.up_r.at[dz])
-        landed(r.rows.at[3, dz], r.low_s.at[dz], r.low_r.at[dz])
-        source, to = (1, after) if j % 2 == 0 else (3, ahead)
-        send(r.rows.at[source, dz], r.rows.at[2, dz], r.far_s.at[dz], r.far_r.at[dz], place.at(), to)
+    for load in loads[2:]:
+        load.wait()
 
     def first_product(j):
-        dz = ORDER[j]
-        landed(r.rows.at[2, dz], r.far_s.at[dz], r.far_r.at[dz])
+        i = ORDER[j]
+        if i:
+            landed(r.rows.at[2, i], r.x_s.at[1, i - 1], r.x_r.at[1, i - 1])
+        landed(r.rows.at[1, i], r.up_s.at[i], r.up_r.at[i])
+        landed(r.rows.at[3, i], r.low_s.at[i], r.low_r.at[i])
         out = jnp.zeros((block, 2 * units), f32)
         for ry in range(NY):
             share = lax.rem(y + NY - ry, NY)
-            out += dot(r.rows[ry, dz], r.gates[part_of(share, part), :])
+            out += dot(r.rows[ry, i], r.gates[part_of(share, part), :])
         gate, up = out[:, :units], out[:, units:]
-        r.hidden[0, dz] = (gate / (1.0 + jnp.exp(-gate)) * up).astype(bf16)
+        r.hidden[0, i] = (gate / (1.0 + jnp.exp(-gate)) * up).astype(bf16)
         for dy, to in ((1, after), (3, ahead)):
             send(
-                r.hidden.at[0, dz], r.hidden.at[dy, dz], r.hid_s.at[dy, dz], r.hid_r.at[dy, dz], place.at(), to
+                r.hidden.at[0, i], r.hidden.at[dy, i], r.hid_s.at[dy, i], r.hid_r.at[dy, i], place.at(), to
             )
 
     def relay_hidden(j):
-        dz = ORDER[j]
+        i = ORDER[j]
         for dy in (1, 3):
-            landed(r.hidden.at[dy, dz], r.hid_s.at[dy, dz], r.hid_r.at[dy, dz])
+            landed(r.hidden.at[dy, i], r.hid_s.at[dy, i], r.hid_r.at[dy, i])
         source, to = (1, after) if j % 2 == 0 else (3, ahead)
-        send(r.hidden.at[source, dz], r.hidden.at[2, dz], r.hid_s.at[2, dz], r.hid_r.at[2, dz], place.at(), to)
+        send(r.hidden.at[source, i], r.hidden.at[2, i], r.hid_s.at[2, i], r.hid_r.at[2, i], place.at(), to)
 
     def second_product(j):
-        dz = ORDER[j]
-        landed(r.hidden.at[2, dz], r.hid_s.at[2, dz], r.hid_r.at[2, dz])
+        i = ORDER[j]
+        landed(r.hidden.at[2, i], r.hid_s.at[2, i], r.hid_r.at[2, i])
         out = jnp.zeros((block, part), f32)
         for ry in range(NY):
-            out += dot(r.hidden[ry, dz], r.down_all[ry])
-        if dz == 0:
+            out += dot(r.hidden[ry, i], r.down_all[ry])
+        if i == 0:
             r.home[0:block, :] = out.astype(bf16)
         else:
-            r.back[dz - 1] = out.astype(bf16)
+            r.back[i - 1] = out.astype(bf16)
             send(
-                r.back.at[dz - 1],
-                r.home.at[cut_of(dz, block)],
-                r.ret_s.at[dz - 1],
-                r.ret_r.at[dz - 1],
-                place.at(dz=NZ - dz),
+                r.back.at[i - 1],
+                r.home.at[cut_of(i, block)],
+                r.ret_s.at[i - 1],
+                r.ret_r.at[i - 1],
+                place.at(dx=NX - i // 2, dk=i % 2),
                 y,
             )
 
-    for j in range(1, steps + 4):
+    def weigh(d):
+        pieces = []
+        for i in range(OCT):
+            code = r.metas[d, 0, expert_at(i), :] + float(d * capacity)
+            pieces.append(jnp.where(number == code, r.metas[d, 1, expert_at(i), :], 0.0))
+        r.spread[cut_of(d, tokens), :] = jnp.concatenate(pieces, axis=0).T.astype(bf16)
+
+    for j in range(steps + 2):
         if j < steps:
-            pass_rows(j)
+            first_product(j)
         if 0 <= j - 1 < steps:
-            relay_rows(j - 1)
+            relay_hidden(j - 1)
         if j == 1:
             for n in range(chunks):
                 r.dense[:, cut_of(n, WIDTH)] = dot(r.feat[...], r.proj[:, cut_of(n, WIDTH)])
-        if 0 <= j - 2 < steps:
-            first_product(j - 2)
-        if 0 <= j - 3 < steps:
-            relay_hidden(j - 3)
-        if j == 4:
+        if j == 2:
             for dy in range(1, NY):
                 landed(r.down_all.at[dy], r.down_s.at[dy - 1], r.down_r.at[dy - 1])
-        if 0 <= j - 4 < steps:
-            second_product(j - 4)
-
-    for dz in ORDER[1:]:
-        landed(r.home.at[cut_of(dz, block)], r.ret_s.at[dz - 1], r.ret_r.at[dz - 1])
-
-    count = NX * tokens
-    for n in range(chunks):
-        r.half[n] = dot(r.spread[:count, :], r.home[:, cut_of(n, WIDTH)]).astype(bf16)
-        send(r.half.at[n], r.half_in.at[n], r.half_s.at[n], r.half_r.at[n], place.at(dk=1), y)
-    for n in range(chunks):
-        r.total[n] = dot(r.spread[count:, :], r.home[:, cut_of(n, WIDTH)])
-        landed(r.half_in.at[n], r.half_s.at[n], r.half_r.at[n])
-        for dx in (2, 1, 3):
-            at = cut_of(dx, tokens)
-            r.third[dx - 1, n] = (r.total[n, at, :] + r.half_in[n, at, :].astype(f32)).astype(bf16)
-            send(
-                r.third.at[dx - 1, n],
-                r.third_in.at[dx - 1, n],
-                r.third_s.at[dx - 1, n],
-                r.third_r.at[dx - 1, n],
-                place.at(dx=dx),
-                y,
-            )
+        if 0 <= j - 2 < steps:
+            second_product(j - 2)
+        if j < steps:
+            weigh(j)
+
+    for i in range(1, OCT):
+        landed(r.home.at[cut_of(i, block)], r.ret_s.at[i - 1], r.ret_r.at[i - 1])
+
+    def sum_hop(n, way, left):
+        d = left if way == 0 else NZ - left
+        here = r.total[n, cut_of(d, tokens), :]
+        if left < NZ // 2 - 1 or (left == NZ // 2 - 1 and n % 2 == way):
+            i = left * chunks + n
+            landed(r.sum_in.at[way, left, n], r.sum_s.at[way, i], r.sum_r.at[way, i])
+            here += r.sum_in[way, left, n].astype(f32)
+        r.sum_out[way, left - 1, n] = here.astype(bf16)
+        i = (left - 1) * chunks + n
+        send(
+            r.sum_out.at[way, left - 1, n],
+            r.sum_in.at[way, left - 1, n],
+            r.sum_s.at[way, i],
+            r.sum_r.at[way, i],
+            place.at(dz=NZ - 1 if way == 0 else 1),
+            y,
+        )
 
     res = Gather(
         place, send, landed, r.residue, tokens, WIDTH, (r.res_s, r.res_r, r.resf_s, r.resf_r)
     )
-    for n in range(chunks + 2):
-        if n < chunks:
-            teacher = r.total[n, :tokens, :] + r.half_in[n, :tokens, :].astype(f32)
-            for dx in (1, 3, 2):
-                landed(r.third_in.at[dx - 1, n], r.third_s.at[dx - 1, n], r.third_r.at[dx - 1, n])
-                teacher += r.third_in[dx - 1, n].astype(f32)
-            cut = cut_of(n, WIDTH)
-            r.residue[slot, cut] = (r.dense[:, cut] - teacher).astype(bf16)
-            res.start(n)
-        if 0 <= n - 1 < chunks:
-            res.relay(n - 1)
-        if 0 <= n - 2 < chunks:
-            res.far(n - 2)
-
+    for wave in range(chunks + NZ // 2 + 2):
+        if wave < chunks:
+            r.total[wave] = dot(r.spread[...], r.home[:, cut_of(wave, WIDTH)])
+        for n in range(chunks):
+            hop = wave - n
+            left = NZ // 2 - hop
+            if hop == 0:
+                sum_hop(n, n % 2, left)
+            elif 0 < hop < NZ // 2:
+                sum_hop(n, 0, left)
+                sum_hop(n, 1, left)
+            elif hop == NZ // 2:
+                teacher = r.total[n, :tokens, :]
+                for way in range(2):
+                    landed(r.sum_in.at[way, 0, n], r.sum_s.at[way, n], r.sum_r.at[way, n])
+                    teacher += r.sum_in[way, 0, n].astype(f32)
+                cut = cut_of(n, WIDTH)
+                r.residue[slot, cut] = (r.dense[:, cut] - teacher).astype(bf16)
+                res.start(n)
+            elif hop == NZ // 2 + 1:
+                res.relay(n)
+            elif hop == NZ // 2 + 2:
+                res.far(n)
     for n in range(features // WIDTH):
         r.part[:, cut_of(n, WIDTH)] = lax.dot_general(
             r.residue[slot, :],
@@ -440,21 +496,19 @@
     buffers = dict(
         proj=(projector.shape, bf16),
         gates=(gate_up.shape, bf16),
-        tok=((OCT * tokens, part), bf16),
+        tok=((2, NZ * tokens, part), bf16),
         metas=(meta.shape, f32),
         select=((block, OCT * tokens), bf16),
         spread=((OCT * tokens, NZ * block), bf16),
-        out=((NZ - 1, block, part), bf16),
+        out=((2, OCT - 1, block, part), bf16),
         rows=((NY, NZ, block, part), bf16),
         hidden=((NY, NZ, block, units), bf16),
         down_all=((NY, units, part), bf16),
         back=((NZ - 1, block, part), bf16),
         home=((NZ * block, part), bf16),
-        half=((chunks, NX * tokens, WIDTH), bf16),
-        half_in=((chunks, NX * tokens, WIDTH), bf16),
-        total=((chunks, NX * tokens, WIDTH), f32),
-        third=((NX - 1, chunks, tokens, WIDTH), bf16),
-        third_in=((NX - 1, chunks, tokens, WIDTH), bf16),
+        total=((chunks, NZ * tokens, WIDTH), f32),
+        sum_out=((2, NZ // 2, chunks, tokens, WIDTH), bf16),
+        sum_in=((2, NZ // 2, chunks, tokens, WIDTH), bf16),
         feat=((tokens, features), bf16),
         dense=((tokens, part), f32),
         slab=((OCT, NZ * piece, tokens), bf16),
@@ -469,18 +523,15 @@
         own_grad=((chunks, NZ, piece, WIDTH), f32),
     )
     flights = dict(
-        meta=(OCT - 1,),
-        tok=(4, 2),
-        tokf=(3, 2),
+        meta=(NZ - 1,),
+        tok=(2, 2 * NZ),
         down=(NY - 1,),
-        z=(NZ - 1,),
-        up=(NZ,),
-        low=(NZ,),
-        far=(NZ,),
-        hid=(NY, NZ),
-        ret=(NZ - 1,),
-        half=(chunks,),
-        third=(NX - 1, chunks),
+        x=(2, OCT - 1),
+        up=(OCT,),
+        low=(OCT,),
+        hid=(NY, OCT),
+        ret=(OCT - 1,),
+        sum=(2, NZ // 2 * chunks),
         slab=(OCT - 1,),
         res=(4, chunks),
         resf=(3, chunks),
@@ -496,7 +547,7 @@
         out_shape=tuple(outputs.values()),
         in_specs=[spec for _, spec in inputs.values()],
         out_specs=[vmem] * len(outputs),
-        scratch_shapes=[pltpu.VMEM(*b) for b in buffers.values()] + [*pairs.values(), dma((4,))],
+        scratch_shapes=[pltpu.VMEM(*b) for b in buffers.values()] + [*pairs.values(), dma((5,))],
         compiler_params=pltpu.CompilerParams(
             collective_id=0, has_side_effects=True, vmem_limit_bytes=60 << 20
         ),
@@ -530,10 +581,10 @@
     experts = lax.axis_size("expert")
     capacity = min(tokens_here, tokens_here * top_count * 9 // (8 * experts))
     position, weight = slot_maps(routes, route_weights, experts)
-    code = jnp.where(position >= 0, position + Place().member() * capacity, -1)
+    code = jnp.where(position >= 0, position, -tokens_here * experts)
     meta = jnp.stack([code.astype(jnp.float32), weight])
-    meta = meta.reshape(2, NX, NZ, 2, tokens_here).transpose(1, 3, 0, 2, 4)
-    meta = meta.reshape(OCT, 2, NZ, tokens_here)
+    meta = meta.reshape(2, NX, NZ, 2, tokens_here).transpose(2, 0, 1, 3, 4)
+    meta = meta.reshape(NZ, 2, OCT, tokens_here)
     gate_up = expert_gate_up.reshape(expert_gate_up.shape[1], -1)
     return layer(
         teacher_in,

time: 225 us -> 203 us (0.902)
  Pallas kernels: 213 us -> 189 us
    pallas_call x1, Pallas kernels: 213 us -> 189 us  [layer(): pl.pallas_call(functools.partial(layer_kernel, names), out_shape=tuple(ou...]
where the time goes in v5:
time: 203 us; the launch traced here: 201 us
  Pallas kernels  189 us (93%)
  local copies, waits for them, and re-layouts  8.95 us (4%)
    pallas_call x1, Pallas kernels, layer(): pl.pallas_call(functools.partial(layer_kernel, names), out_shape=tuple(ou...  189 us
    unnamed x3, local copies, waits for them, and re-layouts  8.29 us

profile of v5, /device:TPU:8, one launch (start us, length us, event | category | flops | bytes accessed | tf_op | source)
XLA Modules:
  0.0 200.8 jit_solution(11506453902117935587)
XLA Ops:
  0.6 0.7 fusion.1
  1.4 0.2 fusion.2
  1.6 0.7 select_reduce_fusion
  2.4 0.7 copy.17
  3.0 4.8 %copy.18 = bf16[512,8,2,256]{3,1,2,0:T(8,128)(2,1)} copy(bf16[512,8,2,256]{3,2,1,0:T(2,128)(2,1)} %bitcast.16) | data formatting | bytes 8388608
  7.9 189.4 %shard_map.104 = (bf16[128,2048]{1,0:T(8,128)(2,1)}, f32[32,1024]{1,0:T(8,128)}) custom-call(bf16[128,4096]{1,0:T(8,128)(2,1)} %refs_0_.1, f32[8,2,8,128]{3,2,1,0:T(8,128)} %bitcast.18, bf16[4096,512]{1,0:T(8,128)(2,1)} %bitcast.15, bf16[256,4096]{1,0:T(8,128)(2,1)} %bitcast.17, bf16[128,2048]{1,0:T(8,128)(2,1)} %refs_4_.1, f32[1,2048]{1,0:T(1,128)} %bitcast.21, ...), custom_call_target="tpu_custom_call" | custom-call | tf_op jit(solution)/shard_map/pallas_call | solution.py:545
  197.3 1.9 copy.21
  199.2 1.6 copy.22
  (2 shorter events, 0.0 us)

commit v6 on v5

--- a/solution.py
+++ b/solution.py
@@ -45,14 +45,14 @@
         return lax.rem(self.x + dx, NX) * 2 + lax.rem(self.k + dk, 2)
 
 
-def meet(place):
+def greet(place):
     barrier = pltpu.get_barrier_semaphore()
     peers = [(place.at(dx=dx, dk=dk), place.y) for dx in range(NX) for dk in range(2) if dx or dk]
     peers += [(place.at(dz=dz), place.y) for dz in range(1, NZ)]
     peers += [(place.at(), lax.rem(place.y + dy, NY)) for dy in range(1, NY)]
     for peer in peers:
         pl.semaphore_signal(barrier, inc=1, device_id=peer, device_id_type=MESH)
-    pl.semaphore_wait(barrier, len(peers))
+    return barrier, len(peers)
 
 
 def cut_of(n, width):
@@ -82,29 +82,20 @@
         at = part_of(self.place.member(dx, dk), self.tokens)
         return self.ref.at[at, cut_of(c, self.width)]
 
-    def start(self, c, own=None):
-        own = self.slot(c) if own is None else own
-        for i, dx, dk in ((1, 1, 0), (3, NX - 1, 0), (0, 0, 1)):
+    def start(self, c):
+        own = self.slot(c)
+        for i, dx, dk in ((2, 2, 0), (1, 1, 0), (3, NX - 1, 0), (0, 0, 1)):
             to = self.place.at(dx=dx, dk=dk)
-            self.send(own, self.slot(c), self.near_s.at[i, c], self.near_r.at[i, c], to, self.place.y)
-
-    def onward(self, c, i):
-        arrived = self.slot(c, NX - i)
-        to = self.place.at(dk=1)
-        self.send(arrived, arrived, self.pass_s.at[i - 1, c], self.pass_r.at[i - 1, c], to, self.place.y)
-
-    def relay(self, c):
-        for i in (1, 3):
-            self.landed(self.slot(c, NX - i), self.near_s.at[i, c], self.near_r.at[i, c])
-            if i == (1 if c % 2 == 0 else 3):
-                arrived = self.slot(c, NX - i)
-                to = self.place.at(dx=i)
-                self.send(arrived, arrived, self.near_s.at[2, c], self.near_r.at[2, c], to, self.place.y)
-            self.onward(c, i)
-
-    def far(self, c):
-        self.landed(self.slot(c, 2), self.near_s.at[2, c], self.near_r.at[2, c])
-        self.onward(c, 2)
+            self.send(own, own, self.near_s.at[i, c], self.near_r.at[i, c], to, self.place.y)
+
+    def onward(self, c):
+        for i in (1, 3, 2):
+            arrived = self.slot(c, NX - i)
+            self.landed(arrived, self.near_s.at[i, c], self.near_r.at[i, c])
+            to = self.place.at(dk=1)
+            self.send(
+                arrived, arrived, self.pass_s.at[i - 1, c], self.pass_r.at[i - 1, c], to, self.place.y
+            )
 
     def finish(self, c):
         self.landed(self.slot(c, 0, 1), self.near_s.at[0, c], self.near_r.at[0, c])
@@ -141,9 +132,13 @@
         pltpu.make_async_copy(r.gate_up, r.gates, r.load.at[3]),
         pltpu.make_async_copy(r.down.at[:, part_of(y, part)], r.down_all.at[0], r.load.at[4]),
     ]
+    barrier, peers = greet(place)
     for load in loads:
         load.start()
-    meet(place)
+    gain = r.gain[...]
+    feat = norm(r.student[...].astype(f32))[1] * gain
+    r.feat[...] = feat.astype(bf16)
+    pl.semaphore_wait(barrier, peers)
     sends = []
 
     def send(*args):
@@ -211,9 +206,6 @@
     r.metas[0] = r.meta[place.z]
     ring_step(0, 1)
 
-    gain = r.gain[...]
-    feat = norm(r.student[...].astype(f32))[1] * gain
-    r.feat[...] = feat.astype(bf16)
     ring_step(0, 2)
 
     for x in range(NX):
@@ -379,6 +371,24 @@
     res = Gather(
         place, send, landed, r.residue, tokens, WIDTH, (r.res_s, r.res_r, r.resf_s, r.resf_r)
     )
+    def sum_rows(n):
+        res.finish(n)
+        grad = dot(r.slabs[...], r.residue[:, cut_of(n, WIDTH)]).reshape(NZ, piece, WIDTH)
+        r.grad[n] = grad.astype(bf16)
+        r.own_grad[n] = grad
+        for dz in (4, 3, 5, 2, 6, 1, 7):
+            send(
+                r.grad.at[n, lax.rem(place.z + dz, NZ)],
+                r.grads.at[dz - 1, n],
+                r.grad_s.at[dz - 1, n],
+                r.grad_r.at[dz - 1, n],
+                place.at(dz=dz),
+                y,
+            )
+
+    for i, (dx, dk) in enumerate(members):
+        at = part_of(place.member(NX - dx, dk), tokens)
+        landed(r.slabs.at[:, at], r.slab_s.at[i], r.slab_r.at[i])
     for wave in range(chunks + NZ // 2 + 2):
         if wave < chunks:
             r.total[wave] = dot(r.spread[...], r.home[:, cut_of(wave, WIDTH)])
@@ -399,9 +409,9 @@
                 r.residue[slot, cut] = (r.dense[:, cut] - teacher).astype(bf16)
                 res.start(n)
             elif hop == NZ // 2 + 1:
-                res.relay(n)
+                res.onward(n)
             elif hop == NZ // 2 + 2:
-                res.far(n)
+                sum_rows(n)
     for n in range(features // WIDTH):
         r.part[:, cut_of(n, WIDTH)] = lax.dot_general(
             r.residue[slot, :],
@@ -419,24 +429,6 @@
             place.at(),
             to,
         )
-
-    for i, (dx, dk) in enumerate(members):
-        at = part_of(place.member(NX - dx, dk), tokens)
-        landed(r.slabs.at[:, at], r.slab_s.at[i], r.slab_r.at[i])
-    for n in range(chunks):
-        res.finish(n)
-        grad = dot(r.slabs[...], r.residue[:, cut_of(n, WIDTH)]).reshape(NZ, piece, WIDTH)
-        r.grad[n] = grad.astype(bf16)
-        r.own_grad[n] = grad
-        for dz in (4, 3, 5, 2, 6, 1, 7):
-            send(
-                r.grad.at[n, lax.rem(place.z + dz, NZ)],
-                r.grads.at[dz - 1, n],
-                r.grad_s.at[dz - 1, n],
-                r.grad_r.at[dz - 1, n],
-                place.at(dz=dz),
-                y,
-            )
 
     own_rows = part_of(y, share_rows)
     feat_grad = r.part[own_rows, :].astype(f32)

time: 203 us -> 205 us (level)
  Pallas kernels: 189 us -> 192 us
    pallas_call x1, Pallas kernels: 189 us -> 192 us  [layer(): pl.pallas_call(functools.partial(layer_kernel, names), out_shape=tuple(ou...]
where the time goes in v6:
time: 205 us; the launch traced here: 203 us
  Pallas kernels  192 us (94%)
  local copies, waits for them, and re-layouts  8.95 us (4%)
    pallas_call x1, Pallas kernels, layer(): pl.pallas_call(functools.partial(layer_kernel, names), out_shape=tuple(ou...  192 us
    unnamed x3, local copies, waits for them, and re-layouts  8.29 us

profile of v6, /device:TPU:8, one launch (start us, length us, event | category | flops | bytes accessed | tf_op | source)
XLA Modules:
  0.0 202.9 jit_solution(1684101602948467294)
XLA Ops:
  0.6 0.7 fusion.1
  1.4 0.2 fusion.2
  1.6 0.7 select_reduce_fusion
  2.4 0.7 copy.17
  3.0 4.8 %copy.18 = bf16[512,8,2,256]{3,1,2,0:T(8,128)(2,1)} copy(bf16[512,8,2,256]{3,2,1,0:T(2,128)(2,1)} %bitcast.16) | data formatting | bytes 8388608
  7.9 191.6 %shard_map.104 = (bf16[128,2048]{1,0:T(8,128)(2,1)}, f32[32,1024]{1,0:T(8,128)}) custom-call(bf16[128,4096]{1,0:T(8,128)(2,1)} %refs_0_.1, f32[8,2,8,128]{3,2,1,0:T(8,128)} %bitcast.18, bf16[4096,512]{1,0:T(8,128)(2,1)} %bitcast.15, bf16[256,4096]{1,0:T(8,128)(2,1)} %bitcast.17, bf16[128,2048]{1,0:T(8,128)(2,1)} %refs_4_.1, f32[1,2048]{1,0:T(1,128)} %bitcast.21, ...), custom_call_target="tpu_custom_call" | custom-call | tf_op jit(solution)/shard_map/pallas_call | solution.py:537
  199.5 1.9 copy.21
  201.4 1.6 copy.22
  (2 shorter events, 0.0 us)

commit v7 on v6

--- a/solution.py
+++ b/solution.py
@@ -13,7 +13,8 @@
 NX, NZ, NY = 4, 8, 4
 OCT = 2 * NX
 WIDTH = 256
-ORDER = (0, 1, 2, 6, 4, 5, 3, 7)
+UNITS = (0, 1, 3, 2, 4, 6, 5, 7)
+DISTANCES = (2, 3, 4, 5, 6, 7, 0, 1)
 
 
 def remote(src, dst, send_sem, recv_sem, expert, share):
@@ -110,23 +111,25 @@
     tokens, features = r.student.shape
     part = r.projector.shape[1]
     units = r.down.shape[0]
-    block = r.rows.shape[2]
+    block = 2 * r.rows.shape[3]
     piece = r.step.shape[0]
     share_rows = tokens // NY
     chunks = part // WIDTH
     f32, bf16 = jnp.float32, jnp.bfloat16
     mine = place.member()
-    steps = len(ORDER)
+    steps = len(UNITS)
     after, ahead = lax.rem(y + 1, NY), lax.rem(y + NY - 1, NY)
 
     capacity = block // NZ
+    fours = NZ // 2
+    rows = block // 2
     far_share = lax.rem(y + 2, NY)
     loads = [
         pltpu.make_async_copy(
-            r.teacher_in.at[:, part_of(y, part)], r.tok.at[0, cut_of(0, tokens)], r.load.at[0]
+            r.teacher_in.at[:, part_of(y, part)], r.tok.at[0, cut_of(DISTANCES.index(0), tokens)], r.load.at[0]
         ),
         pltpu.make_async_copy(
-            r.teacher_in.at[:, part_of(far_share, part)], r.tok.at[1, cut_of(0, tokens)], r.load.at[1]
+            r.teacher_in.at[:, part_of(far_share, part)], r.tok.at[1, cut_of(DISTANCES.index(0), tokens)], r.load.at[1]
         ),
         pltpu.make_async_copy(r.projector, r.proj, r.load.at[2]),
         pltpu.make_async_copy(r.gate_up, r.gates, r.load.at[3]),
@@ -155,7 +158,7 @@
 
     def ring_slot(q, way, hops, c):
         d = hops if way == 0 else (NZ - hops) % NZ
-        return r.tok.at[q, cut_of(d, tokens), cut_of(c, half)]
+        return r.tok.at[q, cut_of(DISTANCES.index(d), tokens), cut_of(c, half)]
 
     def ring_send(q, way, hops, c):
         i = way * NZ + hops * 2 + c
@@ -224,48 +227,57 @@
         landed(r.metas.at[dz], r.meta_s.at[dz - 1], r.meta_r.at[dz - 1])
     ring_step(0, 4)
 
-    number = lax.broadcasted_iota(jnp.int32, (block, tokens), 0).astype(f32)
+    number = lax.broadcasted_iota(jnp.int32, (rows, tokens), 0).astype(f32)
 
     def expert_at(i):
         return pl.ds(place.member(i // 2, i % 2), 1)
 
-    def select_rows(q, i):
-        for d in range(NZ):
-            code = r.metas[d, 0, expert_at(i), :] + float(d * capacity)
-            r.select[:, cut_of(d, tokens)] = jnp.where(number == code, 1.0, 0.0).astype(bf16)
-        picked = dot(r.select[...], r.tok[q]).astype(bf16)
-        if i == 0:
-            r.rows[2 * q, 0] = picked
-        else:
-            r.out[q, i - 1] = picked
-            send(
-                r.out.at[q, i - 1],
-                r.rows.at[2 * q, i],
-                r.x_s.at[q, i - 1],
-                r.x_r.at[q, i - 1],
-                place.at(dx=i // 2, dk=i % 2),
-                y,
-            )
+    def select_rows(q, u):
+        group, dx = u // NX, u % NX
+        for i in range(fours):
+            d = DISTANCES[group * fours + i]
+            pieces = []
+            for dk in range(2):
+                code = r.metas[d, 0, expert_at(2 * dx + dk), :] + float(i * capacity)
+                pieces.append(jnp.where(number == code, 1.0, 0.0))
+            r.select[:, cut_of(i, tokens)] = jnp.concatenate(pieces, axis=0).astype(bf16)
+        picked = dot(r.select[...], r.tok[q, cut_of(group, fours * tokens)])
+        for dk in range(2):
+            if dx or dk:
+                r.out[q, u, dk] = picked[cut_of(dk, rows)].astype(bf16)
+                send(
+                    r.out.at[q, u, dk],
+                    r.rows.at[2 * q, u, dk],
+                    r.x_s.at[q, 2 * u + dk],
+                    r.x_r.at[q, 2 * u + dk],
+                    place.at(dx=dx, dk=dk),
+                    y,
+                )
+            else:
+                r.rows[2 * q, u, dk] = picked[cut_of(dk, rows)].astype(bf16)
+
+    def rows_landed(q, u):
+        for dk in range(2):
+            if u % NX or dk:
+                at = r.rows.at[2 * q, u, dk]
+                landed(at, r.x_s.at[q, 2 * u + dk], r.x_r.at[q, 2 * u + dk])
 
     def pass_rows(j):
-        i = ORDER[j]
-        if i:
-            landed(r.rows.at[0, i], r.x_s.at[0, i - 1], r.x_r.at[0, i - 1])
-        send(r.rows.at[0, i], r.rows.at[1, i], r.up_s.at[i], r.up_r.at[i], place.at(), after)
-        send(r.rows.at[0, i], r.rows.at[3, i], r.low_s.at[i], r.low_r.at[i], place.at(), ahead)
+        u = UNITS[j]
+        rows_landed(0, u)
+        send(r.rows.at[0, u], r.rows.at[1, u], r.up_s.at[u], r.up_r.at[u], place.at(), after)
+        send(r.rows.at[0, u], r.rows.at[3, u], r.low_s.at[u], r.low_r.at[u], place.at(), ahead)
 
     for j in range(steps):
-        select_rows(0, ORDER[j])
-        if j == 0:
-            pass_rows(0)
+        select_rows(0, UNITS[j])
         if j % 2 == 1:
             ring_step(1, (j + 1) // 2)
-        if j >= 3:
-            pass_rows(j - 2)
+        if j >= 1:
+            pass_rows(j - 1)
     for j in range(steps):
-        select_rows(1, ORDER[j])
-        if j < 2:
-            pass_rows(steps - 2 + j)
+        select_rows(1, UNITS[j])
+        if j == 0:
+            pass_rows(steps - 1)
 
     slot = part_of(mine, tokens)
     for i, (dx, dk) in enumerate(members):
@@ -282,15 +294,14 @@
         load.wait()
 
     def first_product(j):
-        i = ORDER[j]
-        if i:
-            landed(r.rows.at[2, i], r.x_s.at[1, i - 1], r.x_r.at[1, i - 1])
+        i = UNITS[j]
+        rows_landed(1, i)
         landed(r.rows.at[1, i], r.up_s.at[i], r.up_r.at[i])
         landed(r.rows.at[3, i], r.low_s.at[i], r.low_r.at[i])
         out = jnp.zeros((block, 2 * units), f32)
         for ry in range(NY):
             share = lax.rem(y + NY - ry, NY)
-            out += dot(r.rows[ry, i], r.gates[part_of(share, part), :])
+            out += dot(r.rows[ry, i].reshape(block, part), r.gates[part_of(share, part), :])
         gate, up = out[:, :units], out[:, units:]
         r.hidden[0, i] = (gate / (1.0 + jnp.exp(-gate)) * up).astype(bf16)
         for dy, to in ((1, after), (3, ahead)):
@@ -299,37 +310,70 @@
             )
 
     def relay_hidden(j):
-        i = ORDER[j]
+        i = UNITS[j]
         for dy in (1, 3):
             landed(r.hidden.at[dy, i], r.hid_s.at[dy, i], r.hid_r.at[dy, i])
         source, to = (1, after) if j % 2 == 0 else (3, ahead)
         send(r.hidden.at[source, i], r.hidden.at[2, i], r.hid_s.at[2, i], r.hid_r.at[2, i], place.at(), to)
 
     def second_product(j):
-        i = ORDER[j]
-        landed(r.hidden.at[2, i], r.hid_s.at[2, i], r.hid_r.at[2, i])
+        u = UNITS[j]
+        dx = u % NX
+        landed(r.hidden.at[2, u], r.hid_s.at[2, u], r.hid_r.at[2, u])
         out = jnp.zeros((block, part), f32)
         for ry in range(NY):
-            out += dot(r.hidden[ry, i], r.down_all[ry])
-        if i == 0:
-            r.home[0:block, :] = out.astype(bf16)
-        else:
-            r.back[i - 1] = out.astype(bf16)
-            send(
-                r.back.at[i - 1],
-                r.home.at[cut_of(i, block)],
-                r.ret_s.at[i - 1],
-                r.ret_r.at[i - 1],
-                place.at(dx=NX - i // 2, dk=i % 2),
-                y,
-            )
-
-    def weigh(d):
+            out += dot(r.hidden[ry, u], r.down_all[ry])
+        for dk in range(2):
+            if dx or dk:
+                r.back[u, dk] = out[cut_of(dk, rows)].astype(bf16)
+                send(
+                    r.back.at[u, dk],
+                    r.home.at[2 * u + dk],
+                    r.ret_s.at[2 * u + dk],
+                    r.ret_r.at[2 * u + dk],
+                    place.at(dx=NX - dx, dk=dk),
+                    y,
+                )
+            else:
+                r.home[2 * u + dk] = out[cut_of(dk, rows)].astype(bf16)
+
+    def weigh(j):
+        group, i = j // fours, j % fours
+        d = DISTANCES[j]
         pieces = []
-        for i in range(OCT):
-            code = r.metas[d, 0, expert_at(i), :] + float(d * capacity)
-            pieces.append(jnp.where(number == code, r.metas[d, 1, expert_at(i), :], 0.0))
-        r.spread[cut_of(d, tokens), :] = jnp.concatenate(pieces, axis=0).T.astype(bf16)
+        for o in range(OCT):
+            code = r.metas[d, 0, expert_at(o), :] + float(i * capacity)
+            pieces.append(jnp.where(number == code, r.metas[d, 1, expert_at(o), :], 0.0))
+        r.spread[group, cut_of(i, tokens), :] = jnp.concatenate(pieces, axis=0).T.astype(bf16)
+
+    def came_home(group):
+        for u in range(group * NX, (group + 1) * NX):
+            for dk in range(2):
+                if u % NX or dk:
+                    landed(r.home.at[2 * u + dk], r.ret_s.at[2 * u + dk], r.ret_r.at[2 * u + dk])
+
+    def combine(group, n):
+        r.total[n, cut_of(group, fours * tokens), :] = dot(
+            r.spread[group], r.home[cut_of(group, OCT), :, cut_of(n, WIDTH)].reshape(NX * block, WIDTH)
+        )
+
+    def sum_hop(n, way, left):
+        d = left if way == 0 else NZ - left
+        here = r.total[n, cut_of(DISTANCES.index(d), tokens), :]
+        if left < NZ // 2 - 1 or (left == NZ // 2 - 1 and n % 2 == way):
+            i = left * chunks + n
+            landed(r.sum_in.at[way, left, n], r.sum_s.at[way, i], r.sum_r.at[way, i])
+            here += r.sum_in[way, left, n].astype(f32)
+        r.sum_out[way, left - 1, n] = here.astype(bf16)
+        i = (left - 1) * chunks + n
+        send(
+            r.sum_out.at[way, left - 1, n],
+            r.sum_in.at[way, left - 1, n],
+            r.sum_s.at[way, i],
+            r.sum_r.at[way, i],
+            place.at(dz=NZ - 1 if way == 0 else 1),
+            y,
+        )
 
     for j in range(steps + 2):
         if j < steps:
@@ -346,27 +390,19 @@
             second_product(j - 2)
         if j < steps:
             weigh(j)
-
-    for i in range(1, OCT):
-        landed(r.home.at[cut_of(i, block)], r.ret_s.at[i - 1], r.ret_r.at[i - 1])
-
-    def sum_hop(n, way, left):
-        d = left if way == 0 else NZ - left
-        here = r.total[n, cut_of(d, tokens), :]
-        if left < NZ // 2 - 1 or (left == NZ // 2 - 1 and n % 2 == way):
-            i = left * chunks + n
-            landed(r.sum_in.at[way, left, n], r.sum_s.at[way, i], r.sum_r.at[way, i])
-            here += r.sum_in[way, left, n].astype(f32)
-        r.sum_out[way, left - 1, n] = here.astype(bf16)
-        i = (left - 1) * chunks + n
-        send(
-            r.sum_out.at[way, left - 1, n],
-            r.sum_in.at[way, left - 1, n],
-            r.sum_s.at[way, i],
-            r.sum_r.at[way, i],
-            place.at(dz=NZ - 1 if way == 0 else 1),
-            y,
-        )
+        if j == NX + 2:
+            came_home(0)
+            for n in range(chunks):
+                combine(0, n)
+                sum_hop(n, n % 2, 4)
+        if j == NX + 3:
+            for n in range(chunks):
+                sum_hop(n, 0, 3)
+                sum_hop(n, 1, 3)
+        if j == NX + 4:
+            for n in range(chunks):
+                sum_hop(n, 0, 2)
+    came_home(1)
 
     res = Gather(
         place, send, landed, r.residue, tokens, WIDTH, (r.res_s, r.res_r, r.resf_s, r.resf_r)
@@ -389,46 +425,46 @@
     for i, (dx, dk) in enumerate(members):
         at = part_of(place.member(NX - dx, dk), tokens)
         landed(r.slabs.at[:, at], r.slab_s.at[i], r.slab_r.at[i])
-    for wave in range(chunks + NZ // 2 + 2):
-        if wave < chunks:
-            r.total[wave] = dot(r.spread[...], r.home[:, cut_of(wave, WIDTH)])
-        for n in range(chunks):
-            hop = wave - n
-            left = NZ // 2 - hop
-            if hop == 0:
-                sum_hop(n, n % 2, left)
-            elif 0 < hop < NZ // 2:
-                sum_hop(n, 0, left)
-                sum_hop(n, 1, left)
-            elif hop == NZ // 2:
-                teacher = r.total[n, :tokens, :]
+    for wave in range(chunks + 4):
+        for n in reversed(range(chunks)):
+            stage = wave - n
+            if stage == 0:
+                combine(1, n)
+                sum_hop(n, 1, 2)
+            elif stage == 1:
+                sum_hop(n, 0, 1)
+                sum_hop(n, 1, 1)
+            elif stage == 2:
+                teacher = r.total[n, cut_of(DISTANCES.index(0), tokens), :]
                 for way in range(2):
                     landed(r.sum_in.at[way, 0, n], r.sum_s.at[way, n], r.sum_r.at[way, n])
                     teacher += r.sum_in[way, 0, n].astype(f32)
                 cut = cut_of(n, WIDTH)
                 r.residue[slot, cut] = (r.dense[:, cut] - teacher).astype(bf16)
                 res.start(n)
-            elif hop == NZ // 2 + 1:
+            elif stage == 3:
                 res.onward(n)
-            elif hop == NZ // 2 + 2:
+            elif stage == 4:
                 sum_rows(n)
-    for n in range(features // WIDTH):
-        r.part[:, cut_of(n, WIDTH)] = lax.dot_general(
-            r.residue[slot, :],
-            r.proj[cut_of(n, WIDTH), :],
-            (((1,), (1,)), ((), ())),
-            preferred_element_type=f32,
-        ).astype(bf16)
-    for dy in (2, 1, 3):
-        to = lax.rem(y + dy, NY)
-        send(
-            r.part.at[part_of(to, share_rows)],
-            r.parts.at[dy - 1],
-            r.part_s.at[dy - 1],
-            r.part_r.at[dy - 1],
-            place.at(),
-            to,
-        )
+        if wave == chunks + 1:
+            for n in range(features // WIDTH):
+                r.part[:, cut_of(n, WIDTH)] = lax.dot_general(
+                    r.residue[slot, :],
+                    r.proj[cut_of(n, WIDTH), :],
+                    (((1,), (1,)), ((), ())),
+                    preferred_element_type=f32,
+                ).astype(bf16)
+            for dy in (2, 1, 3):
+                to = lax.rem(y + dy, NY)
+                send(
+                    r.part.at[part_of(to, share_rows)],
+                    r.parts.at[dy - 1],
+                    r.part_s.at[dy - 1],
+                    r.part_r.at[dy - 1],
+                    place.at(),
+                    to,
+                )
+
 
     own_rows = part_of(y, share_rows)
     feat_grad = r.part[own_rows, :].astype(f32)
@@ -490,14 +526,14 @@
         gates=(gate_up.shape, bf16),
         tok=((2, NZ * tokens, part), bf16),
         metas=(meta.shape, f32),
-        select=((block, OCT * tokens), bf16),
-        spread=((OCT * tokens, NZ * block), bf16),
-        out=((2, OCT - 1, block, part), bf16),
-        rows=((NY, NZ, block, part), bf16),
+        select=((block, NZ // 2 * tokens), bf16),
+        spread=((2, NZ // 2 * tokens, NX * block), bf16),
+        out=((2, OCT, 2, block // 2, part), bf16),
+        rows=((NY, OCT, 2, block // 2, part), bf16),
         hidden=((NY, NZ, block, units), bf16),
         down_all=((NY, units, part), bf16),
-        back=((NZ - 1, block, part), bf16),
-        home=((NZ * block, part), bf16),
+        back=((OCT, 2, block // 2, part), bf16),
+        home=((2 * OCT, block // 2, part), bf16),
         total=((chunks, NZ * tokens, WIDTH), f32),
         sum_out=((2, NZ // 2, chunks, tokens, WIDTH), bf16),
         sum_in=((2, NZ // 2, chunks, tokens, WIDTH), bf16),
@@ -518,11 +554,11 @@
         meta=(NZ - 1,),
         tok=(2, 2 * NZ),
         down=(NY - 1,),
-        x=(2, OCT - 1),
+        x=(2, 2 * OCT),
         up=(OCT,),
         low=(OCT,),
         hid=(NY, OCT),
-        ret=(OCT - 1,),
+        ret=(2 * OCT,),
         sum=(2, NZ // 2 * chunks),
         slab=(OCT - 1,),
         res=(4, chunks),

time: 205 us -> 191 us (0.932); the launches traced: 203 us -> 191 us
  Pallas kernels: 192 us -> 180 us
    pallas_call x1, Pallas kernels: 192 us -> 180 us  [layer(): pl.pallas_call(functools.partial(layer_kernel, names), out_shape=tuple(ou...]
where the time goes in v7:
time: 191 us
  Pallas kernels  180 us (94%)
  local copies, waits for them, and re-layouts  8.95 us (5%)
    pallas_call x1, Pallas kernels, layer(): pl.pallas_call(functools.partial(layer_kernel, names), out_shape=tuple(ou...  180 us
    unnamed x3, local copies, waits for them, and re-layouts  8.29 us

profile of v7, /device:TPU:8, one launch (start us, length us, event | category | flops | bytes accessed | tf_op | source)
XLA Modules:
  0.0 191.2 jit_solution(10782337126191138333)
XLA Ops:
  0.6 0.7 fusion.1
  1.4 0.2 fusion.2
  1.6 0.7 select_reduce_fusion
  2.4 0.7 copy.17
  3.0 4.8 %copy.18 = bf16[512,8,2,256]{3,1,2,0:T(8,128)(2,1)} copy(bf16[512,8,2,256]{3,2,1,0:T(2,128)(2,1)} %bitcast.16) | data formatting | bytes 8388608
  7.9 179.9 %shard_map.104 = (bf16[128,2048]{1,0:T(8,128)(2,1)}, f32[32,1024]{1,0:T(8,128)}) custom-call(bf16[128,4096]{1,0:T(8,128)(2,1)} %refs_0_.1, f32[8,2,8,128]{3,2,1,0:T(8,128)} %bitcast.18, bf16[4096,512]{1,0:T(8,128)(2,1)} %bitcast.15, bf16[256,4096]{1,0:T(8,128)(2,1)} %bitcast.17, bf16[128,2048]{1,0:T(8,128)(2,1)} %refs_4_.1, f32[1,2048]{1,0:T(1,128)} %bitcast.21, ...), custom_call_target="tpu_custom_call" | custom-call | tf_op jit(solution)/shard_map/pallas_call | solution.py:573
  187.8 1.9 copy.21
  189.6 1.6 copy.22
  (2 shorter events, 0.0 us)

commit v8 on v7

--- a/solution.py
+++ b/solution.py
@@ -207,7 +207,25 @@
             to,
         )
     r.metas[0] = r.meta[place.z]
+    number = lax.broadcasted_iota(jnp.int32, (rows, tokens), 0).astype(f32)
+
+    def expert_at(i):
+        return pl.ds(place.member(i // 2, i % 2), 1)
+
+    def weigh(j):
+        group, i = j // fours, j % fours
+        d = DISTANCES[j]
+        pieces = []
+        for o in range(OCT):
+            code = r.metas[d, 0, expert_at(o), :] + float(i * capacity)
+            pieces.append(jnp.where(number == code, r.metas[d, 1, expert_at(o), :], 0.0))
+        r.spread[group, cut_of(i, tokens), :] = jnp.concatenate(pieces, axis=0).T.astype(bf16)
+
     ring_step(0, 1)
+    for dz in range(1, NZ):
+        landed(r.metas.at[dz], r.meta_s.at[dz - 1], r.meta_r.at[dz - 1])
+    for i in range(fours):
+        weigh(i)
 
     ring_step(0, 2)
 
@@ -223,14 +241,9 @@
     ring_step(0, 3)
     loads[1].wait()
     ring_start(1)
-    for dz in range(1, NZ):
-        landed(r.metas.at[dz], r.meta_s.at[dz - 1], r.meta_r.at[dz - 1])
+    for i in range(fours, NZ):
+        weigh(i)
     ring_step(0, 4)
-
-    number = lax.broadcasted_iota(jnp.int32, (rows, tokens), 0).astype(f32)
-
-    def expert_at(i):
-        return pl.ds(place.member(i // 2, i % 2), 1)
 
     def select_rows(q, u):
         group, dx = u // NX, u % NX
@@ -337,15 +350,6 @@
             else:
                 r.home[2 * u + dk] = out[cut_of(dk, rows)].astype(bf16)
 
-    def weigh(j):
-        group, i = j // fours, j % fours
-        d = DISTANCES[j]
-        pieces = []
-        for o in range(OCT):
-            code = r.metas[d, 0, expert_at(o), :] + float(i * capacity)
-            pieces.append(jnp.where(number == code, r.metas[d, 1, expert_at(o), :], 0.0))
-        r.spread[group, cut_of(i, tokens), :] = jnp.concatenate(pieces, axis=0).T.astype(bf16)
-
     def came_home(group):
         for u in range(group * NX, (group + 1) * NX):
             for dk in range(2):
@@ -388,8 +392,6 @@
                 landed(r.down_all.at[dy], r.down_s.at[dy - 1], r.down_r.at[dy - 1])
         if 0 <= j - 2 < steps:
             second_product(j - 2)
-        if j < steps:
-            weigh(j)
         if j == NX + 2:
             came_home(0)
             for n in range(chunks):

time: 191 us -> 191 us (level)
  no operation moved by 1% of the time
where the time goes in v8:
time: 191 us
  Pallas kernels  180 us (94%)
  local copies, waits for them, and re-layouts  8.95 us (5%)
    pallas_call x1, Pallas kernels, layer(): pl.pallas_call(functools.partial(layer_kernel, names), out_shape=tuple(ou...  180 us
    unnamed x3, local copies, waits for them, and re-layouts  8.29 us

profile of v8, /device:TPU:8, one launch (start us, length us, event | category | flops | bytes accessed | tf_op | source)
XLA Modules:
  0.0 190.9 jit_solution(3372381981348978772)
XLA Ops:
  0.6 0.7 fusion.1
  1.4 0.2 fusion.2
  1.6 0.7 select_reduce_fusion
  2.4 0.7 copy.17
  3.0 4.8 %copy.18 = bf16[512,8,2,256]{3,1,2,0:T(8,128)(2,1)} copy(bf16[512,8,2,256]{3,2,1,0:T(2,128)(2,1)} %bitcast.16) | data formatting | bytes 8388608
  7.9 179.5 %shard_map.104 = (bf16[128,2048]{1,0:T(8,128)(2,1)}, f32[32,1024]{1,0:T(8,128)}) custom-call(bf16[128,4096]{1,0:T(8,128)(2,1)} %refs_0_.1, f32[8,2,8,128]{3,2,1,0:T(8,128)} %bitcast.18, bf16[4096,512]{1,0:T(8,128)(2,1)} %bitcast.15, bf16[256,4096]{1,0:T(8,128)(2,1)} %bitcast.17, bf16[128,2048]{1,0:T(8,128)(2,1)} %refs_4_.1, f32[1,2048]{1,0:T(1,128)} %bitcast.21, ...), custom_call_target="tpu_custom_call" | custom-call | tf_op jit(solution)/shard_map/pallas_call | solution.py:575
  187.4 1.9 copy.21
  189.3 1.6 copy.22
  (2 shorter events, 0.0 us)
